TPU v7x, 128 devices: a whole 4x4x4 slice. The times are simulated.
128 devices in a mesh: dp: 16 (over y, x_lo, core), fsdp: 8 (over z, x_hi).
Axes of the slice: x: 4 (x_hi: 2, x_lo: 2; x = x_hi * 2 + x_lo), y: 4, z: 4, core: 2. Of those that a mesh axis runs over, the one named last changes fastest.
Arguments:
- grads: bfloat16 [16, 16, 8, 512, 512], P('dp', None, 'fsdp'), may hold values from -250 to 250
- left_factor: float32 [16, 8, 512, 512], P('dp', 'fsdp'), may hold values from -1 to 8
- right_factor: float32 [16, 8, 512, 512], P('dp', 'fsdp'), may hold values from -1 to 8
- left_basis: bfloat16 [16, 8, 512, 512], P('dp', 'fsdp'), may hold values from -1 to 2
- right_basis: bfloat16 [16, 8, 512, 512], P('dp', 'fsdp'), may hold values from -1 to 2
- first_moment: bfloat16 [16, 8, 512, 512], P('dp', 'fsdp'), may hold values from -0.59765625 to 0.59765625
- second_moment: float32 [16, 8, 512, 512], P('dp', 'fsdp'), may hold values from 0.001 to 0.03
- parameters: bfloat16 [16, 8, 512, 512], P('dp', 'fsdp'), may hold values from -6 to 6
- rotation: int32 [8], P('fsdp'), may hold values from 0 to 15
Outputs:
- parameters_out: bfloat16 [16, 8, 512, 512], P(None, 'fsdp')
- left_out: float32 [16, 8, 512, 512], P('dp', 'fsdp')
- right_out: float32 [16, 8, 512, 512], P('dp', 'fsdp')
- left_basis_out: bfloat16 [16, 8, 512, 512], P('dp', 'fsdp')
- right_basis_out: bfloat16 [16, 8, 512, 512], P('dp', 'fsdp')
- first_out: bfloat16 [16, 8, 512, 512], P('dp', 'fsdp')
- second_out: float32 [16, 8, 512, 512], P('dp', 'fsdp')
All inputs are finite; a program needn't handle non-finite values.
Results may differ from a plain program's by a relative error of at most 0.038.
Values may be sent and summed in bfloat16 or wider, within the bound.
A program may use at most 128 MiB of HBM per device.

v0:
```python
import math

import jax
import jax.numpy as jnp
from jax import lax
from jax.sharding import PartitionSpec as P

ITERS = 2
NEWTON = 3


BETA_MOMENT = 0.95
BETA_SECOND = 0.95
BETA_FACTOR = 0.95
STEP_RATE = 0.05
CLIP_RMS = 0.3
TINY = 1e-08


def shifted(value, axis, steps):
    count = lax.axis_size(axis)
    pairs = [(source, (source + steps) % count) for source in range(count)]
    return lax.ppermute(value, axis, pairs)


def orthonormal(factor, basis_start):
    factor_low = factor.astype(jnp.bfloat16)
    basis_now = basis_start
    identity = jnp.eye(factor.shape[0], dtype=jnp.float32)
    for repeat in range(ITERS):
        image_cols = jnp.dot(factor_low, basis_now, preferred_element_type=jnp.float32)
        magnitude = jnp.abs(image_cols)
        bound = (
            jnp.sqrt(jnp.max(jnp.sum(magnitude, axis=0)) * jnp.max(jnp.sum(magnitude, axis=1)))
            + 1e-06
        )
        iterate = image_cols / bound
        for newton_step in range(NEWTON):
            gram_matrix = jnp.dot(
                iterate.T,
                iterate,
                precision=lax.Precision.HIGHEST,
                preferred_element_type=jnp.float32,
            )
            iterate = jnp.dot(
                iterate,
                1.5 * identity - 0.5 * gram_matrix,
                precision=lax.Precision.HIGHEST,
                preferred_element_type=jnp.float32,
            )
        basis_now = iterate.astype(jnp.bfloat16)
    return basis_now


def block_step(
    grad_mean,
    clip_factor,
    left_old,
    right_old,
    left_basis_old,
    right_basis_old,
    first_old,
    second_old,
    param_old,
):
    grad_low = grad_mean.astype(jnp.bfloat16)
    half_left = jnp.dot(left_basis_old.T, grad_low, preferred_element_type=jnp.float32).astype(
        jnp.bfloat16
    )
    rotated = clip_factor * jnp.dot(half_left, right_basis_old, preferred_element_type=jnp.float32)
    moment = BETA_MOMENT * first_old.astype(jnp.float32) + (1.0 - BETA_MOMENT) * rotated
    second_new = BETA_SECOND * second_old + (1.0 - BETA_SECOND) * rotated * rotated
    direction = (moment / (jnp.sqrt(second_new) + TINY)).astype(jnp.bfloat16)
    half_back = jnp.dot(left_basis_old, direction, preferred_element_type=jnp.float32).astype(
        jnp.bfloat16
    )
    update = jnp.dot(half_back, right_basis_old.T, preferred_element_type=jnp.float32)
    param_new = (param_old.astype(jnp.float32) - STEP_RATE * update).astype(jnp.bfloat16)
    squared_clip = clip_factor * clip_factor
    left_new = BETA_FACTOR * left_old + (1.0 - BETA_FACTOR) * squared_clip * jnp.dot(
        grad_low, grad_low.T, preferred_element_type=jnp.float32
    )
    right_new = BETA_FACTOR * right_old + (1.0 - BETA_FACTOR) * squared_clip * jnp.dot(
        grad_low.T, grad_low, preferred_element_type=jnp.float32
    )
    left_turned = orthonormal(left_new, left_basis_old)
    right_turned = orthonormal(right_new, right_basis_old)
    left_turn = jnp.dot(left_turned.T, left_basis_old, preferred_element_type=jnp.float32).astype(
        jnp.bfloat16
    )
    right_turn = jnp.dot(
        right_basis_old.T, right_turned, preferred_element_type=jnp.float32
    ).astype(jnp.bfloat16)
    half_turned = jnp.dot(
        left_turn, moment.astype(jnp.bfloat16), preferred_element_type=jnp.float32
    ).astype(jnp.bfloat16)
    first_new = jnp.dot(half_turned, right_turn, preferred_element_type=jnp.float32).astype(
        jnp.bfloat16
    )
    return (param_new, left_new, right_new, left_turned, right_turned, first_new, second_new)


def hand_over(wide_state, narrow_state, amount, replicas):
    levels = list(range(replicas.bit_length() - 1))
    for level in levels:
        distance = 2**level
        selected = amount // distance % 2 == 1
        moved_wide = shifted(wide_state.astype(jnp.bfloat16), "dp", distance).astype(
            wide_state.dtype
        )
        moved_narrow = shifted(narrow_state, "dp", distance)
        wide_state = jnp.where(selected, moved_wide, wide_state)
        narrow_state = jnp.where(selected, moved_narrow, narrow_state)
    return (wide_state, narrow_state)


def local(
    grads,
    left_factor,
    right_factor,
    left_basis,
    right_basis,
    first_moment,
    second_moment,
    parameters,
    rotation,
):
    replicas = lax.axis_size("dp")
    columns = lax.axis_size("fsdp")
    amount = rotation[0]
    local_grads = grads[0, :, 0].astype(jnp.float32)
    local_grads = jnp.roll(local_grads, amount, axis=0)
    summed = lax.psum_scatter(
        local_grads.astype(jnp.bfloat16), "dp", scatter_dimension=0, tiled=True
    ).astype(jnp.float32)
    grad_mean = summed[0] * (1.0 / replicas)
    square_sum = lax.psum(jnp.sum(grad_mean * grad_mean), ("dp", "fsdp"))
    entries = grad_mean.size * replicas * columns
    clip_factor = jnp.minimum(1.0, CLIP_RMS * math.sqrt(entries) / jnp.sqrt(square_sum + 1e-06))
    wide_state = jnp.stack([left_factor[0, 0], right_factor[0, 0], second_moment[0, 0]])
    narrow_state = jnp.stack(
        [left_basis[0, 0], right_basis[0, 0], first_moment[0, 0], parameters[0, 0]]
    )
    wide_state, narrow_state = hand_over(wide_state, narrow_state, amount, replicas)
    results = block_step(
        grad_mean,
        clip_factor,
        wide_state[0],
        wide_state[1],
        narrow_state[0],
        narrow_state[1],
        narrow_state[2],
        wide_state[2],
        narrow_state[3],
    )
    param_new, left_new, right_new, left_turned, right_turned, first_new, second_new = results
    gathered = lax.all_gather(param_new[None, None], "dp", axis=0, tiled=True)
    gathered = jnp.roll(gathered, -amount, axis=0)
    return (
        gathered,
        left_new[None, None],
        right_new[None, None],
        left_turned[None, None],
        right_turned[None, None],
        first_new[None, None],
        second_new[None, None],
    )


def solution(mesh):
    return jax.shard_map(
        local,
        mesh=mesh,
        in_specs=(
            P("dp", None, "fsdp", None, None),
            P("dp", "fsdp", None, None),
            P("dp", "fsdp", None, None),
            P("dp", "fsdp", None, None),
            P("dp", "fsdp", None, None),
            P("dp", "fsdp", None, None),
            P("dp", "fsdp", None, None),
            P("dp", "fsdp", None, None),
            P("fsdp"),
        ),
        out_specs=(
            P(None, "fsdp", None, None),
            P("dp", "fsdp", None, None),
            P("dp", "fsdp", None, None),
            P("dp", "fsdp", None, None),
            P("dp", "fsdp", None, None),
            P("dp", "fsdp", None, None),
            P("dp", "fsdp", None, None),
        ),
        check_vma=False,
    )
```

profile of v0, /device:TPU:1, one launch (start us, length us, event | category | flops | bytes accessed | tf_op | source)
XLA Modules:
  0.0 571.0 jit_solution(11447713423687392070)
XLA Ops:
  7.9 8.4 %convert_convert_fusion = bf16[16,512,512]{2,1,0:T(8,128)(2,1)} fusion(s32[]{:T(128)S(6)} %select_n.120, bf16[16,512,512]{2,1,0:T(8,128)(2,1)} %bitcast.144), kind=kLoop, calls=%fused_computation.4 | loop fusion | flops 12582912 | bytes 16777220 | tf_op jit(solution)/shard_map/convert_element_type | solution.py:134
  16.4 3.2 pad_maximum_fusion.1
  19.6 2.6 collective-permute-start
  22.2 1.5 fusion.2
  23.8 55.7 %collective-permute-done = bf16[4,512,512]{2,1,0:T(8,128)(2,1)} collective-permute-done((bf16[4,512,512]{2,1,0:T(8,128)(2,1)}, bf16[4,512,512]{2,1,0:T(8,128)(2,1)}, u32[]{:S(2)}, u32[]{:S(2)}) %collective-permute-start) | collective-permute-done | bytes 2097184 | tf_op jit(solution)/shard_map/ppermute | solution.py:23
  79.5 3.2 broadcast_select_fusion
  82.7 1.0 collective-permute-start.1
  83.7 60.8 %collective-permute-done.4 = bf16[3,512,512]{2,1,0:T(8,128)(2,1)} collective-permute-done((bf16[3,512,512]{2,1,0:T(8,128)(2,1)}, bf16[3,512,512]{2,1,0:T(8,128)(2,1)}, u32[]{:S(2)}, u32[]{:S(2)}) %collective-permute-start.4) | collective-permute-done | bytes 1572896 | tf_op jit(solution)/shard_map/ppermute | solution.py:23
  144.5 3.1 fusion.59
  147.6 0.7 collective-permute-start.5
  148.3 59.9 %collective-permute-done.1 = bf16[4,512,512]{2,1,0:T(8,128)(2,1)} collective-permute-done((bf16[4,512,512]{2,1,0:T(8,128)(2,1)}, bf16[4,512,512]{2,1,0:T(8,128)(2,1)}, u32[]{:S(2)}, u32[]{:S(2)}) %collective-permute-start.1) | collective-permute-done | bytes 2097184 | tf_op jit(solution)/shard_map/ppermute | solution.py:23
  208.2 3.3 broadcast_select_fusion.1
  211.5 0.7 collective-permute-start.2
  212.3 15.8 %collective-permute-done.5 = bf16[3,512,512]{2,1,0:T(8,128)(2,1)} collective-permute-done((bf16[3,512,512]{2,1,0:T(8,128)(2,1)}, bf16[3,512,512]{2,1,0:T(8,128)(2,1)}, u32[]{:S(2)}, u32[]{:S(2)}) %collective-permute-start.5) | collective-permute-done | bytes 1572896 | tf_op jit(solution)/shard_map/ppermute | solution.py:23
  228.1 3.8 fusion.3
  232.0 74.8 %collective-permute-done.6 = bf16[3,512,512]{2,1,0:T(8,128)(2,1)} collective-permute-done((bf16[3,512,512]{2,1,0:T(8,128)(2,1)}, bf16[3,512,512]{2,1,0:T(8,128)(2,1)}, u32[]{:S(2)}, u32[]{:S(2)}) %collective-permute-start.6) | collective-permute-done | bytes 1572896 | tf_op jit(solution)/shard_map/ppermute | solution.py:23
  306.8 4.3 fusion.5
  311.2 1.8 collective-permute-start.7
  313.0 3.1 broadcast_select_fusion.2
  316.1 1.2 collective-permute-start.3
  317.3 31.3 %collective-permute-done.7 = bf16[3,512,512]{2,1,0:T(8,128)(2,1)} collective-permute-done((bf16[3,512,512]{2,1,0:T(8,128)(2,1)}, bf16[3,512,512]{2,1,0:T(8,128)(2,1)}, u32[]{:S(2)}, u32[]{:S(2)}) %collective-permute-start.7) | collective-permute-done | bytes 1572896 | tf_op jit(solution)/shard_map/ppermute | solution.py:23
  348.6 5.6 convert_select_fusion
  354.2 1.9 multiply_reduce_fusion
  356.1 37.4 %collective-permute-done.3 = bf16[4,512,512]{2,1,0:T(8,128)(2,1)} collective-permute-done((bf16[4,512,512]{2,1,0:T(8,128)(2,1)}, bf16[4,512,512]{2,1,0:T(8,128)(2,1)}, u32[]{:S(2)}, u32[]{:S(2)}) %collective-permute-start.3) | collective-permute-done | bytes 2097184 | tf_op jit(solution)/shard_map/ppermute | solution.py:23
  393.5 3.1 broadcast_select_fusion.3
  396.7 66.5 %psum.7 = f32[]{:T(128)} all-reduce(f32[]{:T(128)} %multiply_reduce_fusion), channel_id=1, replica_groups=mesh['dp'=16,'fsdp'=8] {'dp','fsdp'}, use_global_device_ids=true, to_apply=%region_2.3 | all-reduce | flops 1 | bytes 8 | tf_op jit(solution)/shard_map/psum | solution.py:137
  463.9 3.1 convolution_multiply_fusion.15
  467.0 3.9 fusion.12
  470.9 1.7 fusion.10
  472.6 1.0 copy-done.4
  473.6 2.5 abs_reduce_fusion.6
  478.6 3.5 select_subtract_fusion.11
  482.1 1.9 fusion.31
  484.0 1.9 select_subtract_fusion.10
  485.9 1.8 fusion.60
  487.7 1.9 select_subtract_fusion.9
  489.6 2.3 convolution_convert_fusion.9
  491.9 1.4 abs_reduce_fusion.4
  495.8 1.7 fusion.8
  497.6 1.0 copy-done.6
  498.5 2.5 abs_reduce_fusion.2
  503.5 3.6 select_subtract_fusion.5
  507.2 1.9 fusion.33
  509.1 1.9 select_subtract_fusion.4
  510.9 1.8 fusion.62
  512.8 2.1 select_subtract_fusion.3
  514.9 1.8 convolution_convert_fusion.7
  516.7 1.4 abs_reduce_fusion
  520.7 3.5 select_subtract_fusion.8
  524.2 1.9 select_subtract_fusion.2
  526.1 1.9 fusion.32
  528.0 1.9 select_subtract_fusion.7
  529.9 1.8 fusion.61
  531.8 2.1 select_subtract_fusion.6
  533.8 2.6 convolution_convert_fusion.8
  536.5 1.9 fusion.34
  538.4 1.9 select_subtract_fusion.1
  540.2 1.8 fusion.63
  542.1 1.9 select_subtract_fusion
  544.0 2.9 convolution_convert_fusion.6
  546.9 3.2 convolution_convert_fusion.2
  550.1 3.0 fusion.4
  553.0 2.4 fusion.22
  555.5 8.3 %fusion = bf16[16,1,512,512]{3,2,1,0:T(8,128)(2,1)} fusion(s32[]{:T(128)S(6)} %select_n.130, bf16[16,1,512,512]{3,2,1,0:T(8,128)(2,1)} %bitcast.145), kind=kLoop, calls=%fused_computation.5 | loop fusion | flops 4194304 | bytes 16777220 | tf_op jit(solution)/shard_map/jit(_roll_dynamic)/concatenate | solution.py:158
  (39 shorter events, 5.2 us)
Async XLA Ops:
  7.2 347.0 %reduce-scatter.2.cloned.1.call-start = ((), (), s32[]{:S(2)}) async-start(), calls=%async_computation.1 | async-start | bytes 8912896 | tf_op jit(solution)/shard_map/reduce_scatter | solution.py:133
  16.3 539.2 %all-gather.3.cloned.1.call-start = ((), (), s32[]{:S(2)}) async-start(), calls=%async_computation.2 | async-start | bytes 8912896 | tf_op jit(solution)/shard_map/all_gather | solution.py:157
  16.4 5.9 %copy-start = (f32[1,1,512,512]{3,2,1,0:T(8,128)S(1)}, f32[1,1,512,512]{3,2,1,0:T(8,128)}, u32[]{:S(2)}) copy-start(f32[1,1,512,512]{3,2,1,0:T(8,128)} %param.15) | copy-start | bytes 3145732
  16.4 5.9 %copy-start.1 = (f32[1,1,512,512]{3,2,1,0:T(8,128)S(1)}, f32[1,1,512,512]{3,2,1,0:T(8,128)}, u32[]{:S(2)}) copy-start(f32[1,1,512,512]{3,2,1,0:T(8,128)} %param.11) | copy-start | bytes 3145732
  16.4 5.8 %copy-start.2 = (f32[1,1,512,512]{3,2,1,0:T(8,128)S(1)}, f32[1,1,512,512]{3,2,1,0:T(8,128)}, u32[]{:S(2)}) copy-start(f32[1,1,512,512]{3,2,1,0:T(8,128)} %param.10) | copy-start | bytes 3145732
  19.6 59.9 %collective-permute-start = (bf16[4,512,512]{2,1,0:T(8,128)(2,1)}, bf16[4,512,512]{2,1,0:T(8,128)(2,1)}, u32[]{:S(2)}, u32[]{:S(2)}) collective-permute-start(bf16[4,512,512]{2,1,0:T(8,128)(2,1)} %pad_maximum_fusion.1), channel_id=1, source_target_pairs={{0,8},{8,16},{16,24},{24,32},{32,40},{40,48},{48,56},{56,64},{64,7... | collective-permute-start | bytes 6291464 | tf_op jit(solution)/shard_map/ppermute | solution.py:23
  23.7 120.8 %collective-permute-start.4 = (bf16[3,512,512]{2,1,0:T(8,128)(2,1)}, bf16[3,512,512]{2,1,0:T(8,128)(2,1)}, u32[]{:S(2)}, u32[]{:S(2)}) collective-permute-start(bf16[3,512,512]{2,1,0:T(8,128)(2,1)} %fusion.2), channel_id=1, source_target_pairs={{0,8},{8,16},{16,24},{24,32},{32,40},{40,48},{48,56},{56,64},{64,7... | collective-permute-start | bytes 4718600 | tf_op jit(solution)/shard_map/ppermute | solution.py:23
  82.7 125.5 %collective-permute-start.1 = (bf16[4,512,512]{2,1,0:T(8,128)(2,1)}, bf16[4,512,512]{2,1,0:T(8,128)(2,1)}, u32[]{:S(2)}, u32[]{:S(2)}) collective-permute-start(bf16[4,512,512]{2,1,0:T(8,128)(2,1)} %broadcast_select_fusion), channel_id=1, source_target_pairs={{0,16},{8,24},{16,32},{24,40},{32,48},{40,56},{48,64},{56,72},{64,... | collective-permute-start | bytes 6291464 | tf_op jit(solution)/shard_map/ppermute | solution.py:23
  147.6 80.5 %collective-permute-start.5 = (bf16[3,512,512]{2,1,0:T(8,128)(2,1)}, bf16[3,512,512]{2,1,0:T(8,128)(2,1)}, u32[]{:S(2)}, u32[]{:S(2)}) collective-permute-start(bf16[3,512,512]{2,1,0:T(8,128)(2,1)} %fusion.59), channel_id=1, source_target_pairs={{0,16},{8,24},{16,32},{24,40},{32,48},{40,56},{48,64},{56,72},{64,... | collective-permute-start | bytes 4718600 | tf_op jit(solution)/shard_map/ppermute | solution.py:23
  211.5 101.4 %collective-permute-start.2 = (bf16[4,512,512]{2,1,0:T(8,128)(2,1)}, bf16[4,512,512]{2,1,0:T(8,128)(2,1)}, u32[]{:S(2)}, u32[]{:S(2)}) collective-permute-start(bf16[4,512,512]{2,1,0:T(8,128)(2,1)} %broadcast_select_fusion.1), channel_id=1, source_target_pairs={{0,32},{8,40},{16,48},{24,56},{32,64},{40,72},{48,80},{56,88},{64,... | collective-permute-start | bytes 6291464 | tf_op jit(solution)/shard_map/ppermute | solution.py:23
  231.9 75.0 %collective-permute-start.6 = (bf16[3,512,512]{2,1,0:T(8,128)(2,1)}, bf16[3,512,512]{2,1,0:T(8,128)(2,1)}, u32[]{:S(2)}, u32[]{:S(2)}) collective-permute-start(bf16[3,512,512]{2,1,0:T(8,128)(2,1)} %fusion.3), channel_id=1, source_target_pairs={{0,32},{8,40},{16,48},{24,56},{32,64},{40,72},{48,80},{56,88},{64,... | collective-permute-start | bytes 4718600 | tf_op jit(solution)/shard_map/ppermute | solution.py:23
  311.2 37.4 %collective-permute-start.7 = (bf16[3,512,512]{2,1,0:T(8,128)(2,1)}, bf16[3,512,512]{2,1,0:T(8,128)(2,1)}, u32[]{:S(2)}, u32[]{:S(2)}) collective-permute-start(bf16[3,512,512]{2,1,0:T(8,128)(2,1)} %fusion.5), channel_id=1, source_target_pairs={{0,64},{8,72},{16,80},{24,88},{32,96},{40,104},{48,112},{56,120},{... | collective-permute-start | bytes 4718600 | tf_op jit(solution)/shard_map/ppermute | solution.py:23
  316.1 77.4 %collective-permute-start.3 = (bf16[4,512,512]{2,1,0:T(8,128)(2,1)}, bf16[4,512,512]{2,1,0:T(8,128)(2,1)}, u32[]{:S(2)}, u32[]{:S(2)}) collective-permute-start(bf16[4,512,512]{2,1,0:T(8,128)(2,1)} %broadcast_select_fusion.2), channel_id=1, source_target_pairs={{0,64},{8,72},{16,80},{24,88},{32,96},{40,104},{48,112},{56,120},{... | collective-permute-start | bytes 6291464 | tf_op jit(solution)/shard_map/ppermute | solution.py:23
  396.7 70.3 %copy-start.3 = (f32[3,512,512]{2,1,0:T(8,128)S(1)}, f32[3,512,512]{2,1,0:T(8,128)}, u32[]{:S(2)}) copy-start(f32[3,512,512]{2,1,0:T(8,128)} %convert_select_fusion) | copy-start | bytes 9437188
  472.6 1.0 copy-start.4
  478.6 3.5 copy-start.10
  489.6 2.3 copy-start.5
  497.5 1.0 copy-start.6
  503.5 3.6 copy-start.11
  514.8 1.9 copy-start.7
  520.7 3.5 copy-start.9
  524.2 1.9 copy-start.8
Sparse Core Ops, SparseCore 0:
  16.4 164.0 reduce-scatter.1
  471.0 49.7 all-gather.2
where the time goes:
time: 579 us; the launch traced here: 571 us
  waiting for transfers between devices  336 us (58%)
  matrix products  76.6 us (13%)
  blocking collectives  66.5 us (11%)
  other arithmetic  60.1 us (10%)
  between operations  21.6 us (4%)
  starting transfers between devices  8.33 us (1%)
    ppermute x8, waiting for transfers between devices, shifted(): return lax.ppermute(value, axis, pairs)  336 us
    psum x1, blocking collectives, local(): square_sum = lax.psum(jnp.sum(grad_mean * grad_mean), ('dp', 'fsdp'))  66.5 us
    dot_general x12, matrix products, orthonormal(): jnp.dot(iterate.T, iterate, precision=lax.Precision.HIGHEST, preferred_el...  27.8 us
    dot_general x12, matrix products, orthonormal(): jnp.dot(iterate, 1.5 * identity - 0.5 * gram_matrix, precision=lax.Precis...  24.6 us
    select_n x4, other arithmetic, hand_over(): narrow_state = jnp.where(selected, moved_narrow, narrow_state)  12.7 us
    convert_element_type x4, other arithmetic, hand_over(): wide_state.astype(jnp.bfloat16)  12.7 us
  transfers between devices with their start and end apart: 10, of which 7 were waited for; matrix products, arithmetic and copies ran while one was open for 19% of the time, Pallas kernels for 0%

commit v1 on v0

v1 whole, which is shorter than its diff:
```python
import math

import jax
import jax.numpy as jnp
from jax import lax
from jax.experimental import pallas as pl
from jax.experimental.pallas import tpu as pltpu
from jax.sharding import PartitionSpec as P

ITERS = 2
NEWTON = 3
SIDE = 512
REPLICAS = 16
COLUMNS = 8
CHUNK = SIDE // REPLICAS

BETA_MOMENT = 0.95
BETA_SECOND = 0.95
BETA_FACTOR = 0.95
STEP_RATE = 0.05
CLIP_RMS = 0.3
TINY = 1e-08

Y_ROWS = 208
X_ROWS = SIDE - Y_ROWS
YS = pl.ds(0, Y_ROWS)
XS = pl.ds(Y_ROWS, X_ROWS)

MESH = pl.DeviceIdType.MESH
BF = jnp.bfloat16
F32 = jnp.float32


def place():
    me = lax.axis_index("dp")
    return me, me // 4, me // 2 % 2, me % 2


def index_of(y, x, core):
    return y % 4 * 4 + x % 2 * 2 + core % 2


def remote(src, dst, send, recv, **where):
    return pltpu.make_async_remote_copy(
        src_ref=src, dst_ref=dst, send_sem=send, recv_sem=recv, device_id=where, device_id_type=MESH
    )


def greet_replicas(barrier, me):
    def greet(step, carry):
        pl.semaphore_signal(
            barrier, inc=1, device_id={"dp": (me + step) % REPLICAS}, device_id_type=MESH
        )
        return carry

    lax.fori_loop(1, REPLICAS, greet, 0)


def reduce_kernel(
    grads,
    low_out,
    total_out,
    own,
    twin,
    x_in,
    y_in,
    y_late,
    x_late,
    tile,
    tile2,
    local_sem,
    core_send,
    core_recv,
    send,
    recv,
    ring_send,
    ring_recv,
    column_send,
    column_recv,
):
    me, y, x, core = place()
    column = lax.axis_index("fsdp")
    barrier = pltpu.get_barrier_semaphore()
    greet_replicas(barrier, me)

    def greet_column(step, carry):
        pl.semaphore_signal(
            barrier, inc=1, device_id={"fsdp": (column + step) % COLUMNS}, device_id_type=MESH
        )
        return carry

    lax.fori_loop(1, COLUMNS, greet_column, 0)

    order = [(2, 1), (1, 1), (3, 1), (0, 1), (2, 0), (1, 0), (3, 0), (0, 0)]
    loads, swaps = {}, {}
    for dy, dx in order:
        k = dy * 2 + dx
        loads[dy, dx] = pltpu.make_async_copy(
            grads.at[index_of(y + dy, x + dx, core)], own.at[k], local_sem.at[k]
        )
        loads[dy, dx].start()
    pl.semaphore_wait(barrier, REPLICAS - 1 + COLUMNS - 1)
    for dy, dx in order:
        k = dy * 2 + dx
        swaps[dy, dx] = remote(
            grads.at[index_of(y + dy, x + dx, core + 1)],
            twin.at[k],
            core_send.at[k],
            core_recv.at[k],
            dp=index_of(y, x, core + 1),
        )
        swaps[dy, dx].start()

    x_first, y_first, y_second = {}, {}, {}
    used = 0
    for dy, dx in order:
        k = dy * 2 + dx
        loads[dy, dx].wait()
        swaps[dy, dx].wait_recv()
        own[k] = own[k] + twin[k]
        if dx == 1:
            x_first[dy] = remote(
                own.at[k, XS], x_in.at[dy], send.at[used], recv.at[used], dp=index_of(y, x + 1, core)
            )
            x_first[dy].start()
            used += 1
        if dy:
            y_first[dy, dx] = remote(
                own.at[k, YS],
                y_in.at[dy - 1, dx],
                send.at[used],
                recv.at[used],
                dp=index_of(y + dy, x, core),
            )
            y_first[dy, dx].start()
            used += 1
    for dy in (2, 1, 3):
        x_first[dy].wait_recv()
        own[dy * 2, XS] = own[dy * 2, XS] + x_in[dy]
        y_second[dy] = remote(
            own.at[dy * 2, XS],
            y_late.at[dy - 1],
            send.at[used],
            recv.at[used],
            dp=index_of(y + dy, x, core),
        )
        y_second[dy].start()
        used += 1
    for dy in (2, 1, 3):
        y_first[dy, 1].wait_recv()
    own[1, YS] = (
        (own[1, YS].astype(F32) + y_in[0, 1].astype(F32))
        + (y_in[1, 1].astype(F32) + y_in[2, 1].astype(F32))
    ).astype(BF)
    x_second = remote(
        own.at[1, YS], x_late, send.at[used], recv.at[used], dp=index_of(y, x + 1, core)
    )
    x_second.start()
    for dy in (2, 1, 3):
        y_first[dy, 0].wait_recv()
    x_first[0].wait_recv()
    for dy in (2, 1, 3):
        y_second[dy].wait_recv()
    mean_x = (
        (own[0, XS].astype(F32) + x_in[0].astype(F32))
        + (y_late[0].astype(F32) + y_late[1].astype(F32))
        + y_late[2].astype(F32)
    ) * (1.0 / REPLICAS)
    low_out[XS] = mean_x.astype(BF)
    x_second.wait_recv()
    mean_y = (
        (own[0, YS].astype(F32) + x_late[...].astype(F32))
        + (y_in[0, 0].astype(F32) + y_in[1, 0].astype(F32))
        + y_in[2, 0].astype(F32)
    ) * (1.0 / REPLICAS)
    low_out[YS] = mean_y.astype(BF)
    squares = jnp.sum((mean_x * mean_x).reshape(X_ROWS // 8, 8, SIDE), axis=0) + jnp.sum(
        (mean_y * mean_y).reshape(Y_ROWS // 8, 8, SIDE), axis=0
    )
    tile[0] = (squares[:, :128] + squares[:, 128:256]) + (squares[:, 256:384] + squares[:, 384:])

    def ring_copy(step):
        return remote(
            tile.at[0],
            tile.at[step],
            ring_send.at[step],
            ring_recv.at[step],
            dp=(me + step) % REPLICAS,
        )

    def column_copy(step):
        return remote(
            tile2.at[0],
            tile2.at[step],
            column_send.at[step],
            column_recv.at[step],
            fsdp=(column + step) % COLUMNS,
        )

    lax.fori_loop(1, REPLICAS, lambda step, carry: (ring_copy(step).start(), carry)[1], 0)
    lax.fori_loop(1, REPLICAS, lambda step, carry: (ring_copy(step).wait_recv(), carry)[1], 0)
    tile2[0] = jnp.sum(tile[...], axis=0)
    lax.fori_loop(1, COLUMNS, lambda step, carry: (column_copy(step).start(), carry)[1], 0)
    lax.fori_loop(1, COLUMNS, lambda step, carry: (column_copy(step).wait_recv(), carry)[1], 0)
    total_out[...] = jnp.sum(tile2[...], axis=0)

    lax.fori_loop(1, REPLICAS, lambda step, carry: (ring_copy(step).wait_send(), carry)[1], 0)
    lax.fori_loop(1, COLUMNS, lambda step, carry: (column_copy(step).wait_send(), carry)[1], 0)
    for group in (swaps, x_first, y_first, y_second):
        for copy in group.values():
            copy.wait_send()
    x_second.wait_send()


def reduce_grads(grads):
    vmem = pl.BlockSpec(memory_space=pltpu.VMEM)
    dma = pltpu.SemaphoreType.DMA
    return pl.pallas_call(
        reduce_kernel,
        out_shape=(
            jax.ShapeDtypeStruct((SIDE, SIDE), BF),
            jax.ShapeDtypeStruct((8, 128), F32),
        ),
        in_specs=[pl.BlockSpec(memory_space=pl.ANY)],
        out_specs=(vmem, vmem),
        scratch_shapes=[
            pltpu.VMEM((8, SIDE, SIDE), BF),
            pltpu.VMEM((8, SIDE, SIDE), BF),
            pltpu.VMEM((4, X_ROWS, SIDE), BF),
            pltpu.VMEM((3, 2, Y_ROWS, SIDE), BF),
            pltpu.VMEM((3, X_ROWS, SIDE), BF),
            pltpu.VMEM((Y_ROWS, SIDE), BF),
            pltpu.VMEM((REPLICAS, 8, 128), F32),
            pltpu.VMEM((COLUMNS, 8, 128), F32),
            dma((8,)),
            dma((8,)),
            dma((8,)),
            dma((14,)),
            dma((14,)),
            dma((REPLICAS,)),
            dma((REPLICAS,)),
            dma((COLUMNS,)),
            dma((COLUMNS,)),
        ],
        compiler_params=pltpu.CompilerParams(
            collective_id=0, has_side_effects=True, vmem_limit_bytes=40 * 2**20
        ),
        cost_estimate=pl.CostEstimate(flops=0, bytes_accessed=16 * 2**20, transcendentals=0),
        name="reduce_grads",
    )(grads)


def spread_kernel(
    param,
    state,
    rotation,
    params_out,
    state_out,
    gathered,
    rolled,
    local_sem,
    send,
    recv,
    core_send,
    core_recv,
    first_send,
    first_recv,
    second_send,
    second_recv,
):
    me, y, x, core = place()
    barrier = pltpu.get_barrier_semaphore()
    greet_replicas(barrier, me)
    keep = pltpu.make_async_copy(param, params_out.at[me], local_sem.at[0])
    keep.start()
    pl.semaphore_wait(barrier, REPLICAS - 1)

    beside = index_of(y, x + 1, core)
    twin = index_of(y, x, core + 1)
    used = [0]
    used_core = [0]

    def pass_on(src, owner, rows, target):
        copy = remote(
            src, params_out.at[owner, rows], send.at[used[0]], recv.at[used[0]], dp=target
        )
        used[0] += 1
        copy.start()
        return copy

    twins = []

    def to_twin(src, owner, rows):
        k = used_core[0]
        used_core[0] += 1
        copy = remote(src, params_out.at[owner, rows], core_send.at[k], core_recv.at[k], dp=twin)
        copy.start()
        twins.append(copy)

    copies = []
    x_own = pass_on(param.at[YS], me, YS, beside)
    y_own = {dy: pass_on(param.at[XS], me, XS, index_of(y + dy, x, core)) for dy in (2, 1, 3)}
    x_same = pass_on(param.at[XS], me, XS, beside)
    y_same = {dy: pass_on(param.at[YS], me, YS, index_of(y + dy, x, core)) for dy in (2, 1, 3)}
    to_twin(param, me, pl.ds(0, SIDE))

    def first_copy(step):
        return remote(
            state.at[(me + step) % REPLICAS],
            gathered.at[me],
            first_send.at[step],
            first_recv.at[step],
            dp=(me + step) % REPLICAS,
        )

    def second_copy(step):
        return remote(
            rolled.at[(me + step) % REPLICAS],
            state_out.at[me],
            second_send.at[step],
            second_recv.at[step],
            dp=(me + step) % REPLICAS,
        )

    lax.fori_loop(1, REPLICAS, lambda step, carry: (first_copy(step).start(), carry)[1], 0)
    mine = pltpu.make_async_copy(state.at[me], gathered.at[me], local_sem.at[1])
    mine.start()

    x_own.wait_recv()
    y_pair = {
        dy: pass_on(params_out.at[beside, YS], beside, YS, index_of(y + dy, x, core))
        for dy in (2, 1, 3)
    }
    to_twin(params_out.at[beside, YS], beside, YS)
    x_pass = {}
    for dy in (2, 1, 3):
        y_own[dy].wait_recv()
        owner = index_of(y - dy, x, core)
        x_pass[dy] = pass_on(params_out.at[owner, XS], owner, XS, beside)
        to_twin(params_out.at[owner, XS], owner, XS)
    x_same.wait_recv()
    to_twin(params_out.at[beside, XS], beside, XS)
    for dy in (2, 1, 3):
        y_same[dy].wait_recv()
        owner = index_of(y - dy, x, core)
        to_twin(params_out.at[owner, YS], owner, YS)
    for dy in (2, 1, 3):
        y_pair[dy].wait_recv()
        owner = index_of(y - dy, x + 1, core)
        to_twin(params_out.at[owner, YS], owner, YS)
    for dy in (2, 1, 3):
        x_pass[dy].wait_recv()
        owner = index_of(y - dy, x + 1, core)
        to_twin(params_out.at[owner, XS], owner, XS)

    lax.fori_loop(1, REPLICAS, lambda step, carry: (first_copy(step).wait_recv(), carry)[1], 0)
    mine.wait()
    shift = rotation[0]

    def roll(step, carry):
        rolled[step] = gathered[(step + REPLICAS - shift) % REPLICAS]
        return carry

    lax.fori_loop(0, REPLICAS, roll, 0)
    lax.fori_loop(1, REPLICAS, lambda step, carry: (second_copy(step).start(), carry)[1], 0)
    back = pltpu.make_async_copy(rolled.at[me], state_out.at[me], local_sem.at[2])
    back.start()
    keep.wait()
    for copy in twins:
        copy.wait()
    for group in (y_own, y_same, y_pair, x_pass):
        for copy in group.values():
            copy.wait_send()
    x_own.wait_send()
    x_same.wait_send()
    lax.fori_loop(1, REPLICAS, lambda step, carry: (first_copy(step).wait_send(), carry)[1], 0)
    lax.fori_loop(1, REPLICAS, lambda step, carry: (second_copy(step).wait(), carry)[1], 0)
    back.wait()


def spread(param, state, rotation):
    hbm = pl.BlockSpec(memory_space=pl.ANY)
    dma = pltpu.SemaphoreType.DMA
    rows = state.shape[1]
    return pl.pallas_call(
        spread_kernel,
        out_shape=(
            jax.ShapeDtypeStruct((REPLICAS, SIDE, SIDE), BF),
            jax.ShapeDtypeStruct(state.shape, BF),
        ),
        in_specs=[hbm, hbm, pl.BlockSpec(memory_space=pltpu.SMEM)],
        out_specs=(hbm, hbm),
        scratch_shapes=[
            pltpu.VMEM((REPLICAS, rows, SIDE), BF),
            pltpu.VMEM((REPLICAS, rows, SIDE), BF),
            dma((3,)),
            dma((14,)),
            dma((14,)),
            dma((15,)),
            dma((15,)),
            dma((REPLICAS,)),
            dma((REPLICAS,)),
            dma((REPLICAS,)),
            dma((REPLICAS,)),
        ],
        compiler_params=pltpu.CompilerParams(
            collective_id=1, has_side_effects=True, vmem_limit_bytes=40 * 2**20
        ),
        cost_estimate=pl.CostEstimate(flops=0, bytes_accessed=32 * 2**20, transcendentals=0),
        name="spread",
    )(param, state, rotation)


def dot(a, b):
    return jnp.dot(a, b, preferred_element_type=F32)


def orthonormal(factor, basis_start):
    factor_low = factor.astype(BF)
    basis_now = basis_start
    for repeat in range(ITERS):
        image = dot(factor_low, basis_now)
        magnitude = jnp.abs(image)
        bound = (
            jnp.sqrt(jnp.max(jnp.sum(magnitude, axis=0)) * jnp.max(jnp.sum(magnitude, axis=1)))
            + 1e-06
        )
        iterate = image * (1.0 / bound)
        for newton_step in range(NEWTON):
            low = iterate.astype(BF)
            gram = dot(low.T, low).astype(BF)
            iterate = 1.5 * iterate - 0.5 * dot(low, gram)
        basis_now = iterate.astype(BF)
    return basis_now


def local(
    grads,
    left_factor,
    right_factor,
    left_basis,
    right_basis,
    first_moment,
    second_moment,
    parameters,
    rotation,
):
    grad_low, squares = reduce_grads(grads[0, :, 0])
    square_sum = jnp.sum(squares)
    entries = SIDE * SIDE * REPLICAS * COLUMNS
    clip_factor = jnp.minimum(1.0, CLIP_RMS * math.sqrt(entries) / jnp.sqrt(square_sum + 1e-06))
    left_old, right_old = left_basis[0, 0], right_basis[0, 0]
    half_left = dot(left_old.T, grad_low).astype(BF)
    rotated = clip_factor * dot(half_left, right_old)
    moment = BETA_MOMENT * first_moment[0, 0].astype(F32) + (1.0 - BETA_MOMENT) * rotated
    second_new = BETA_SECOND * second_moment[0, 0] + (1.0 - BETA_SECOND) * rotated * rotated
    direction = (moment / (jnp.sqrt(second_new) + TINY)).astype(BF)
    half_back = dot(left_old, direction).astype(BF)
    update = dot(half_back, right_old.T)
    param_new = (parameters[0, 0].astype(F32) - STEP_RATE * update).astype(BF)
    weight = (1.0 - BETA_FACTOR) * (clip_factor * clip_factor)
    left_new = BETA_FACTOR * left_factor[0, 0] + weight * dot(grad_low, grad_low.T)
    right_new = BETA_FACTOR * right_factor[0, 0] + weight * dot(grad_low.T, grad_low)
    left_turned = orthonormal(left_new, left_old)
    right_turned = orthonormal(right_new, right_old)
    left_turn = dot(left_turned.T, left_old).astype(BF)
    right_turn = dot(right_old.T, right_turned).astype(BF)
    first_new = dot(dot(left_turn, moment.astype(BF)).astype(BF), right_turn).astype(BF)
    state = jnp.concatenate(
        [
            value.astype(BF).reshape(REPLICAS, CHUNK, SIDE)
            for value in (left_new, right_new, second_new, left_turned, right_turned, first_new)
        ],
        axis=1,
    )
    gathered, moved = spread(param_new, state, rotation)
    outs = [
        moved[:, CHUNK * k : CHUNK * (k + 1)].reshape(1, 1, SIDE, SIDE) for k in range(6)
    ]
    return (
        gathered[:, None],
        outs[0].astype(F32),
        outs[1].astype(F32),
        outs[3],
        outs[4],
        outs[5],
        outs[2].astype(F32),
    )


def solution(mesh):
    state = P("dp", "fsdp", None, None)
    return jax.shard_map(
        local,
        mesh=mesh,
        in_specs=(P("dp", None, "fsdp", None, None),) + (state,) * 7 + (P("fsdp"),),
        out_specs=(P(None, "fsdp", None, None),) + (state,) * 6,
        check_vma=False,
    )
```

time: 579 us -> 267 us (0.46); the launches traced: 571 us -> 266 us
  waiting for transfers between devices: 336 us -> 0 us
  Pallas kernels: 0 us -> 162 us
  blocking collectives: 66.5 us -> 0 us
  other arithmetic: 60.1 us -> 8.71 us
  between operations: 21.6 us -> 7.69 us
  local copies, waits for them, and re-layouts: 1.98 us -> 13.6 us
  starting transfers between devices: 8.33 us -> 0 us
    ppermute x8 -> x0, waiting for transfers between devices: 336 us -> none  [shifted(): return lax.ppermute(value, axis, pairs)]
    pallas_call x0 -> x2, Pallas kernels: none -> 162 us  [the longest x1 109 us: spread(): pl.pallas_call(spread_kernel, out_shape=(jax.ShapeDtypeStruct((REPLICAS,...]
    psum x1 -> x0, blocking collectives: 66.5 us -> none  [local(): square_sum = lax.psum(jnp.sum(grad_mean * grad_mean), ('dp', 'fsdp'))]
    select_n x5 -> x0, other arithmetic: 18.3 us -> none  [the longest x4 12.7 us: hand_over(): narrow_state = jnp.where(selected, moved_narrow, narrow_state)]
    convert_element_type x5 -> x3, other arithmetic: 21.1 us -> 3.31 us  [the longest x1 1.1 us: local(): outs[2].astype(F32)]
    unnamed x24 -> x20, local copies, waits for them, and re-layouts: 1.98 us -> 12.2 us
    concatenate x1 -> x0, other arithmetic: 8.28 us -> none  [local(): gathered = jnp.roll(gathered, -amount, axis=0)]
    ppermute x8 -> x0, starting transfers between devices: 8.25 us -> none  [shifted(): return lax.ppermute(value, axis, pairs)]
  transfers between devices with their start and end apart: 10 -> 0, of which waited for: 7 -> 0; matrix products, arithmetic and copies ran while one was open for 19% -> 0% of each run, Pallas kernels for 0% -> 0%
where the time goes in v1:
time: 267 us; the launch traced here: 266 us
  Pallas kernels  162 us (61%)
  matrix products  73.9 us (28%)
  local copies, waits for them, and re-layouts  13.6 us (5%)
  other arithmetic  8.71 us (3%)
  between operations  7.69 us (3%)
    pallas_call x1, Pallas kernels, spread(): pl.pallas_call(spread_kernel, out_shape=(jax.ShapeDtypeStruct((REPLICAS,...  109 us
    dot_general x22, matrix products, dot(): return jnp.dot(a, b, preferred_element_type=F32)  73.9 us
    pallas_call x1, Pallas kernels, reduce_grads(): pl.pallas_call(reduce_kernel, out_shape=(jax.ShapeDtypeStruct((SIDE, SIDE...  53.6 us
    unnamed x20, local copies, waits for them, and re-layouts  12.2 us

profile of v1, /device:TPU:1, one launch (start us, length us, event | category | flops | bytes accessed | tf_op | source)
XLA Modules:
  0.0 266.2 jit_solution(15754104393251426483)
XLA Ops:
  0.6 0.0 copy-start
  1.4 0.0 copy-start.1
  1.4 3.4 %copy-done.1 = bf16[1,16,1,512,512]{4,3,2,1,0:T(8,128)(2,1)S(1)} copy-done((bf16[1,16,1,512,512]{4,3,2,1,0:T(8,128)(2,1)S(1)}, bf16[1,16,1,512,512]{4,3,2,1,0:T(8,128)(2,1)}, u32[]{:S(2)}) %copy-start.1) | copy-done | bytes 8388632
  4.7 0.0 copy-start.2
  4.7 53.6 %reduce_grads.1 = (bf16[512,512]{1,0:T(8,128)(2,1)S(1)}, f32[8,128]{1,0:T(8,128)S(1)}) custom-call(bf16[16,512,512]{2,1,0:T(8,128)(2,1)S(1)} %bitcast.87), custom_call_target="tpu_custom_call" | custom-call | bytes 16777216 | tf_op jit(solution)/shard_map/reduce_grads/pallas_call | solution.py:218
  58.3 0.0 copy-start.3
  58.3 0.6 reduce_sum.81
  59.6 0.0 copy-done.2
  59.6 0.5 fusion.17
  60.1 1.7 fusion.16
  61.8 0.0 copy-done
  61.8 0.0 copy-done.3
  61.8 3.0 %fusion.68 = (bf16[512,512]{1,0:T(8,128)(2,1)S(1)}, f32[512,512]{1,0:T(8,128)}) fusion(f32[1,1,512,512]{3,2,1,0:T(8,128)} %param.15, bf16[1,1,512,512]{3,2,1,0:T(8,128)(2,1)S(1)} %copy-done.3, bf16[512,512]{1,0:T(8,128)(2,1)S(1)} %get-tuple-element.12, bf16[1,1,512,512]{3,2,1,0:T(8,128)(2,1)S(1)} %copy-done, f32[]{:T(128)S(6)} %min.3), kind=kOutput, calls=%fused_computation.98 | convolution fusion | flops 538705920 | bytes 4194308 | tf_op jit(solution)/shard_map/dot_general | solution.py:415
  64.8 3.0 %fusion.15.param = bf16[512,512]{1,0:T(8,128)(2,1)S(1)} fusion(f32[512,512]{1,0:T(8,128)} %get-tuple-element.37, bf16[1,1,512,512]{3,2,1,0:T(8,128)(2,1)} %param.14, bf16[1,1,512,512]{3,2,1,0:T(8,128)(2,1)} %param.16, bf16[1,1,512,512]{3,2,1,0:T(8,128)(2,1)S(1)} %copy-done.3, bf16[1,1,512,512]{3,2,1,0:T(8,128)(2,1)S(1)} %copy-done, ...), kind=kOutput, calls=%fused_computation.33 | convolution fusion | flops 540803072 | bytes 4718592 | tf_op jit(solution)/shard_map/dot_general | solution.py:415
  67.9 1.4 abs_reduce_fusion.6
  69.3 0.6 reduce_max.72
  69.9 0.6 reduce_max.73
  71.9 4.4 %fusion.11 = f32[512,512]{1,0:T(8,128)} fusion(f32[512,512]{1,0:T(8,128)} %get-tuple-element.38, f32[]{:T(128)S(6)} %div.20), kind=kOutput, calls=%fused_computation.25 | convolution fusion | flops 539230208 | bytes 2097156 | tf_op jit(solution)/shard_map/dot_general | solution.py:415
  76.3 4.4 %fusion.10 = f32[512,512]{1,0:T(8,128)} fusion(f32[512,512]{1,0:T(8,128)} %fusion.11), kind=kOutput, calls=%fused_computation.23 | convolution fusion | flops 538443776 | bytes 2097152 | tf_op jit(solution)/shard_map/dot_general | solution.py:415
  80.7 4.2 %fusion.18 = bf16[512,512]{1,0:T(8,128)(2,1)} fusion(f32[512,512]{1,0:T(8,128)} %fusion.10), kind=kOutput, calls=%fused_computation.36 | convolution fusion | flops 538705920 | bytes 1572864 | tf_op jit(solution)/shard_map/dot_general | solution.py:415
  85.0 2.5 abs_reduce_fusion.4
  87.4 0.6 reduce_max.74
  88.0 0.6 reduce_max.75
  90.0 4.4 %fusion.8 = f32[512,512]{1,0:T(8,128)} fusion(f32[512,512]{1,0:T(8,128)} %get-tuple-element.39, f32[]{:T(128)S(6)} %div.21), kind=kOutput, calls=%fused_computation.19 | convolution fusion | flops 539230208 | bytes 2097156 | tf_op jit(solution)/shard_map/dot_general | solution.py:415
  94.4 4.4 %fusion.7 = f32[512,512]{1,0:T(8,128)} fusion(f32[512,512]{1,0:T(8,128)} %fusion.8), kind=kOutput, calls=%fused_computation.17 | convolution fusion | flops 538443776 | bytes 2097152 | tf_op jit(solution)/shard_map/dot_general | solution.py:415
  98.9 4.2 %fusion.19 = bf16[512,512]{1,0:T(8,128)(2,1)} fusion(f32[512,512]{1,0:T(8,128)} %fusion.7), kind=kOutput, calls=%fused_computation.37 | convolution fusion | flops 538705920 | bytes 1572864 | tf_op jit(solution)/shard_map/dot_general | solution.py:415
  103.1 3.0 %convolution_convert_fusion.2 = bf16[512,512]{1,0:T(8,128)(2,1)} fusion(bf16[512,512]{1,0:T(8,128)(2,1)} %fusion.19, f32[512,512]{1,0:T(8,128)} %get-tuple-element.37, bf16[1,1,512,512]{3,2,1,0:T(8,128)(2,1)} %param.14, bf16[1,1,512,512]{3,2,1,0:T(8,128)(2,1)S(1)} %copy-done), kind=kOutput, calls=%fused_computation.42 | convolution fusion | flops 538705920 | bytes 3145728 | tf_op jit(solution)/shard_map/dot_general | solution.py:415
  106.2 1.4 abs_reduce_fusion.2
  107.6 0.6 reduce_max.76
  108.2 0.6 reduce_max.77
  110.2 4.3 %fusion.5 = f32[512,512]{1,0:T(8,128)} fusion(f32[512,512]{1,0:T(8,128)} %get-tuple-element.40, f32[]{:T(128)S(6)} %div.22), kind=kOutput, calls=%fused_computation.13 | convolution fusion | flops 539230208 | bytes 2097156 | tf_op jit(solution)/shard_map/dot_general | solution.py:415
  114.5 4.4 %fusion.4 = f32[512,512]{1,0:T(8,128)} fusion(f32[512,512]{1,0:T(8,128)} %fusion.5), kind=kOutput, calls=%fused_computation.11 | convolution fusion | flops 538443776 | bytes 2097152 | tf_op jit(solution)/shard_map/dot_general | solution.py:415
  118.9 4.1 %fusion.20 = bf16[512,512]{1,0:T(8,128)(2,1)} fusion(f32[512,512]{1,0:T(8,128)} %fusion.4), kind=kOutput, calls=%fused_computation.38 | convolution fusion | flops 538705920 | bytes 1572864 | tf_op jit(solution)/shard_map/dot_general | solution.py:415
  123.0 2.5 abs_reduce_fusion
  125.5 0.6 reduce_max.78
  126.1 0.6 reduce_max.79
  128.1 4.3 %fusion.2 = f32[512,512]{1,0:T(8,128)} fusion(f32[512,512]{1,0:T(8,128)} %get-tuple-element.41, f32[]{:T(128)S(6)} %div.23), kind=kOutput, calls=%fused_computation.7 | convolution fusion | flops 539230208 | bytes 2097156 | tf_op jit(solution)/shard_map/dot_general | solution.py:415
  132.4 4.4 %fusion.1 = f32[512,512]{1,0:T(8,128)} fusion(f32[512,512]{1,0:T(8,128)} %fusion.2), kind=kOutput, calls=%fused_computation.5 | convolution fusion | flops 538443776 | bytes 2097152 | tf_op jit(solution)/shard_map/dot_general | solution.py:415
  136.8 4.1 %fusion.21 = bf16[512,512]{1,0:T(8,128)(2,1)} fusion(f32[512,512]{1,0:T(8,128)} %fusion.1), kind=kOutput, calls=%fused_computation.39 | convolution fusion | flops 538705920 | bytes 1572864 | tf_op jit(solution)/shard_map/dot_general | solution.py:415
  140.9 3.0 %convolution_convert_fusion = bf16[512,512]{1,0:T(8,128)(2,1)} fusion(bf16[512,512]{1,0:T(8,128)(2,1)} %convolution_convert_fusion.2, bf16[512,512]{1,0:T(8,128)(2,1)} %fusion.21, bf16[1,1,512,512]{3,2,1,0:T(8,128)(2,1)S(1)} %copy-done.3), kind=kOutput, calls=%fused_computation.40 | convolution fusion | flops 537395200 | bytes 2097152 | tf_op jit(solution)/shard_map/dot_general | solution.py:415
  143.9 0.0 copy-start.4
  143.9 0.0 copy-start.6
  144.0 0.0 copy-start.5
  144.1 0.9 copy-done.4
  145.0 0.1 copy-done.6
  145.2 0.1 copy-done.5
  145.3 108.7 %spread.1 = (bf16[16,512,512]{2,1,0:T(8,128)(2,1)}, bf16[16,192,512]{2,1,0:T(8,128)(2,1)S(1)}) custom-call(bf16[512,512]{1,0:T(8,128)(2,1)S(1)} %fusion.15.param, bf16[16,192,512]{2,1,0:T(8,128)(2,1)S(1)} %constant_dynamic-update-slice_fusion.state, s32[1]{0:T(128)S(6)} %copy.23.rotation), custom_call_target="tpu_custom_call" | custom-call | bytes 33554432 | tf_op jit(solution)/shard_map/spread/pallas_call | solution.py:385
  254.0 1.3 fusion.82
  255.4 1.1 convert.7
  256.5 1.1 convert.6
  257.6 1.1 convert.5
  258.7 7.5 %copy.24 = bf16[16,1,512,512]{3,2,1,0:T(8,128)(2,1)} copy(bf16[16,1,512,512]{3,2,1,0:T(8,128)(2,1)} %bitcast.88) | data formatting | bytes 16777216
  (6 shorter events, 0.2 us)
Async XLA Ops:
  0.6 61.2 %copy-start = (bf16[1,1,512,512]{3,2,1,0:T(8,128)(2,1)S(1)}, bf16[1,1,512,512]{3,2,1,0:T(8,128)(2,1)}, u32[]{:S(2)}) copy-start(bf16[1,1,512,512]{3,2,1,0:T(8,128)(2,1)} %param.12) | copy-start | bytes 1572868
  1.4 3.4 %copy-start.1 = (bf16[1,16,1,512,512]{4,3,2,1,0:T(8,128)(2,1)S(1)}, bf16[1,16,1,512,512]{4,3,2,1,0:T(8,128)(2,1)}, u32[]{:S(2)}) copy-start(bf16[1,16,1,512,512]{4,3,2,1,0:T(8,128)(2,1)} %param.9) | copy-start | bytes 25165828
  4.7 54.9 %copy-start.2 = (f32[1,1,512,512]{3,2,1,0:T(8,128)S(1)}, f32[1,1,512,512]{3,2,1,0:T(8,128)}, u32[]{:S(2)}) copy-start(f32[1,1,512,512]{3,2,1,0:T(8,128)} %param.11) | copy-start | bytes 3145732
  58.3 3.5 %copy-start.3 = (bf16[1,1,512,512]{3,2,1,0:T(8,128)(2,1)S(1)}, bf16[1,1,512,512]{3,2,1,0:T(8,128)(2,1)}, u32[]{:S(2)}) copy-start(bf16[1,1,512,512]{3,2,1,0:T(8,128)(2,1)} %param.13) | copy-start | bytes 1572868
  143.9 1.0 copy-start.4
  143.9 1.2 copy-start.6
  144.0 1.4 copy-start.5

commit v2 on v1

v2 whole, which is shorter than its diff:
```python
import math

import jax
import jax.numpy as jnp
from jax import lax
from jax.experimental import pallas as pl
from jax.experimental.pallas import tpu as pltpu
from jax.sharding import PartitionSpec as P

ITERS = 2
NEWTON = 3
SIDE = 512
REPLICAS = 16
COLUMNS = 8
CHUNK = SIDE // REPLICAS

BETA_MOMENT = 0.95
BETA_SECOND = 0.95
BETA_FACTOR = 0.95
STEP_RATE = 0.05
CLIP_RMS = 0.3
TINY = 1e-08

Y_ROWS = 208
X_ROWS = SIDE - Y_ROWS
YS = pl.ds(0, Y_ROWS)
XS = pl.ds(Y_ROWS, X_ROWS)

MESH = pl.DeviceIdType.MESH
BF = jnp.bfloat16
F32 = jnp.float32


def place():
    me = lax.axis_index("dp")
    return me, me // 4, me // 2 % 2, me % 2


def index_of(y, x, core):
    return y % 4 * 4 + x % 2 * 2 + core % 2


def remote(src, dst, send, recv, **where):
    return pltpu.make_async_remote_copy(
        src_ref=src, dst_ref=dst, send_sem=send, recv_sem=recv, device_id=where, device_id_type=MESH
    )


def greet_replicas(barrier, me):
    def greet(step, carry):
        pl.semaphore_signal(
            barrier, inc=1, device_id={"dp": (me + step) % REPLICAS}, device_id_type=MESH
        )
        return carry

    lax.fori_loop(1, REPLICAS, greet, 0)


def nn(a, b):
    return jnp.dot(a, b, preferred_element_type=F32)


def nt(a, b):
    return lax.dot_general(a, b, (((1,), (1,)), ((), ())), preferred_element_type=F32)


def tn(a, b):
    return lax.dot_general(a, b, (((0,), (0,)), ((), ())), preferred_element_type=F32)


def each(count, act):
    lax.fori_loop(1, count, lambda step, carry: (act(step), carry)[1], 0)


def chunked(value):
    return value.reshape(REPLICAS, CHUNK, SIDE)


def image_step(factor, basis, iterate, low):
    image = nn(factor, basis)
    magnitude = jnp.abs(image)
    bound = (
        jnp.sqrt(jnp.max(jnp.sum(magnitude, axis=0)) * jnp.max(jnp.sum(magnitude, axis=1)))
        + 1e-06
    )
    scaled = image * (1.0 / bound)
    iterate[...] = scaled
    low[...] = scaled.astype(BF)


def newton_step(iterate, low, gram):
    gram[...] = nt(low[...], low[...]).astype(BF)
    value = 1.5 * iterate[...] - 0.5 * nn(gram[...], low[...])
    iterate[...] = value
    low[...] = value.astype(BF)


def step_kernel(
    grads,
    left_hbm,
    right_hbm,
    second_hbm,
    left_basis_hbm,
    right_basis_hbm,
    first_hbm,
    param_hbm,
    rotation,
    params_out,
    wide_out,
    narrow_out,
    own,
    twin,
    x_in,
    y_in,
    y_late,
    x_late,
    tile,
    tile2,
    left_old,
    right_old,
    second_old,
    left_basis,
    right_basis,
    first_old,
    param_old,
    grad_low,
    rotated,
    moment_low,
    left_iter,
    right_iter,
    left_low,
    right_low,
    left_gram,
    right_gram,
    wide,
    narrow,
    wide_in,
    narrow_in,
    wide_rolled,
    narrow_rolled,
    local_sem,
    load_sem,
    core_send,
    core_recv,
    send,
    recv,
    ring_send,
    ring_recv,
    column_send,
    column_recv,
    ag_send,
    ag_recv,
    twin_send,
    twin_recv,
    wide_send,
    wide_recv,
    wide_send2,
    wide_recv2,
    narrow_send,
    narrow_recv,
    narrow_send2,
    narrow_recv2,
):
    me, y, x, core = place()
    column = lax.axis_index("fsdp")
    barrier = pltpu.get_barrier_semaphore()
    greet_replicas(barrier, me)
    def greet_column(step, carry):
        pl.semaphore_signal(
            barrier, inc=1, device_id={"fsdp": (column + step) % COLUMNS}, device_id_type=MESH
        )
        return carry

    lax.fori_loop(1, COLUMNS, greet_column, 0)

    order = [(2, 1), (1, 1), (3, 1), (0, 1), (2, 0), (1, 0), (3, 0), (0, 0)]
    loads, swaps = {}, {}
    for dy, dx in order:
        k = dy * 2 + dx
        loads[dy, dx] = pltpu.make_async_copy(
            grads.at[index_of(y + dy, x + dx, core)], own.at[k], local_sem.at[k]
        )
        loads[dy, dx].start()
    pl.semaphore_wait(barrier, REPLICAS - 1 + COLUMNS - 1)
    for dy, dx in order:
        k = dy * 2 + dx
        swaps[dy, dx] = remote(
            grads.at[index_of(y + dy, x + dx, core + 1)],
            twin.at[k],
            core_send.at[k],
            core_recv.at[k],
            dp=index_of(y, x, core + 1),
        )
        swaps[dy, dx].start()

    state_loads = [
        pltpu.make_async_copy(source, target, load_sem.at[k])
        for k, (source, target) in enumerate(
            (
                (left_basis_hbm, left_basis),
                (right_basis_hbm, right_basis),
                (first_hbm, first_old),
                (second_hbm, second_old),
                (left_hbm, left_old),
                (right_hbm, right_old),
                (param_hbm, param_old),
            )
        )
    ]
    for load in state_loads:
        load.start()

    x_first, y_first, y_second = {}, {}, {}
    used = 0
    for dy, dx in order:
        k = dy * 2 + dx
        loads[dy, dx].wait()
        swaps[dy, dx].wait_recv()
        own[k] = own[k] + twin[k]
        if dx == 1:
            x_first[dy] = remote(
                own.at[k, XS], x_in.at[dy], send.at[used], recv.at[used], dp=index_of(y, x + 1, core)
            )
            x_first[dy].start()
            used += 1
        if dy:
            y_first[dy, dx] = remote(
                own.at[k, YS],
                y_in.at[dy - 1, dx],
                send.at[used],
                recv.at[used],
                dp=index_of(y + dy, x, core),
            )
            y_first[dy, dx].start()
            used += 1
    for dy in (2, 1, 3):
        x_first[dy].wait_recv()
        own[dy * 2, XS] = own[dy * 2, XS] + x_in[dy]
        y_second[dy] = remote(
            own.at[dy * 2, XS],
            y_late.at[dy - 1],
            send.at[used],
            recv.at[used],
            dp=index_of(y + dy, x, core),
        )
        y_second[dy].start()
        used += 1
    for dy in (2, 1, 3):
        y_first[dy, 1].wait_recv()
    own[1, YS] = (
        (own[1, YS].astype(F32) + y_in[0, 1].astype(F32))
        + (y_in[1, 1].astype(F32) + y_in[2, 1].astype(F32))
    ).astype(BF)
    x_second = remote(
        own.at[1, YS], x_late, send.at[used], recv.at[used], dp=index_of(y, x + 1, core)
    )
    x_second.start()
    for dy in (2, 1, 3):
        y_first[dy, 0].wait_recv()
    x_first[0].wait_recv()
    for dy in (2, 1, 3):
        y_second[dy].wait_recv()
    mean_x = (
        (own[0, XS].astype(F32) + x_in[0].astype(F32))
        + (y_late[0].astype(F32) + y_late[1].astype(F32))
        + y_late[2].astype(F32)
    ) * (1.0 / REPLICAS)
    grad_low[XS] = mean_x.astype(BF)
    x_second.wait_recv()
    mean_y = (
        (own[0, YS].astype(F32) + x_late[...].astype(F32))
        + (y_in[0, 0].astype(F32) + y_in[1, 0].astype(F32))
        + y_in[2, 0].astype(F32)
    ) * (1.0 / REPLICAS)
    grad_low[YS] = mean_y.astype(BF)
    squares = jnp.sum((mean_x * mean_x).reshape(X_ROWS // 8, 8, SIDE), axis=0) + jnp.sum(
        (mean_y * mean_y).reshape(Y_ROWS // 8, 8, SIDE), axis=0
    )
    tile[0] = (squares[:, :128] + squares[:, 128:256]) + (squares[:, 256:384] + squares[:, 384:])

    def ring_copy(step):
        return remote(
            tile.at[0],
            tile.at[step],
            ring_send.at[step],
            ring_recv.at[step],
            dp=(me + step) % REPLICAS,
        )

    def column_copy(step):
        return remote(
            tile2.at[0],
            tile2.at[step],
            column_send.at[step],
            column_recv.at[step],
            fsdp=(column + step) % COLUMNS,
        )

    each(REPLICAS, lambda step: ring_copy(step).start())
    for load in state_loads:
        load.wait()
    half_left = tn(left_basis[...], grad_low[...]).astype(BF)
    rotated[...] = nn(half_left, right_basis[...])
    each(REPLICAS, lambda step: ring_copy(step).wait_recv())
    tile2[0] = jnp.sum(tile[...], axis=0)
    each(COLUMNS, lambda step: column_copy(step).start())
    left_iter[...] = nt(grad_low[...], grad_low[...])
    right_iter[...] = tn(grad_low[...], grad_low[...])
    each(COLUMNS, lambda step: column_copy(step).wait_recv())
    square_sum = jnp.sum(jnp.sum(tile2[...], axis=0))
    entries = SIDE * SIDE * REPLICAS * COLUMNS
    clip_factor = jnp.minimum(1.0, CLIP_RMS * math.sqrt(entries) / jnp.sqrt(square_sum + 1e-06))

    def state_copy(source, target, sends, recvs, step):
        there = (me + step) % REPLICAS
        return remote(
            source.at[there], target.at[me], sends.at[step], recvs.at[step], dp=there
        )

    def wide_copy(step):
        return state_copy(wide, wide_in, wide_send, wide_recv, step)

    def narrow_copy(step):
        return state_copy(narrow, narrow_in, narrow_send, narrow_recv, step)

    def wide_copy2(step):
        return state_copy(wide_rolled, wide_out, wide_send2, wide_recv2, step)

    def narrow_copy2(step):
        return state_copy(narrow_rolled, narrow_out, narrow_send2, narrow_recv2, step)

    weight = (1.0 - BETA_FACTOR) * (clip_factor * clip_factor)
    left_new = (BETA_FACTOR * left_old[...] + weight * left_iter[...]).astype(BF)
    right_new = (BETA_FACTOR * right_old[...] + weight * right_iter[...]).astype(BF)
    wide[:, 0:CHUNK] = chunked(left_new)
    wide[:, CHUNK : 2 * CHUNK] = chunked(right_new)
    turned = clip_factor * rotated[...]
    moment = BETA_MOMENT * first_old[...].astype(F32) + (1.0 - BETA_MOMENT) * turned
    second_new = BETA_SECOND * second_old[...] + (1.0 - BETA_SECOND) * turned * turned
    wide[:, 2 * CHUNK : 3 * CHUNK] = chunked(second_new.astype(BF))
    moment_low[...] = moment.astype(BF)
    direction = (moment / (jnp.sqrt(second_new) + TINY)).astype(BF)
    each(REPLICAS, lambda step: wide_copy(step).start())
    wide_in[me] = wide[me]

    half_back = nn(left_basis[...], direction).astype(BF)
    update = nt(half_back, right_basis[...])
    params_out[me] = (param_old[...].astype(F32) - STEP_RATE * update).astype(BF)

    beside = index_of(y, x + 1, core)
    other = index_of(y, x, core + 1)
    counts = [0, 0]
    copies = []

    def pass_on(owner, rows, target):
        k = counts[0]
        counts[0] += 1
        view = params_out.at[owner, rows]
        copy = remote(view, view, ag_send.at[k], ag_recv.at[k], dp=target)
        copy.start()
        copies.append(copy)
        return copy

    twins = []

    def to_twin(owner, rows):
        k = counts[1]
        counts[1] += 1
        view = params_out.at[owner, rows]
        copy = remote(view, view, twin_send.at[k], twin_recv.at[k], dp=other)
        copy.start()
        twins.append(copy)

    x_own = pass_on(me, YS, beside)
    y_own = {dy: pass_on(me, XS, index_of(y + dy, x, core)) for dy in (2, 1, 3)}
    x_same = pass_on(me, XS, beside)
    y_same = {dy: pass_on(me, YS, index_of(y + dy, x, core)) for dy in (2, 1, 3)}
    to_twin(me, pl.ds(0, SIDE))

    for repeat in range(ITERS):
        left_start = left_basis if repeat == 0 else left_low
        right_start = right_basis if repeat == 0 else right_low
        image_step(
            wide[:, 0:CHUNK].reshape(SIDE, SIDE), left_start[...], left_iter, left_low
        )
        image_step(
            wide[:, CHUNK : 2 * CHUNK].reshape(SIDE, SIDE), right_start[...], right_iter, right_low
        )
        for newton in range(NEWTON):
            newton_step(left_iter, left_low, left_gram)
            newton_step(right_iter, right_low, right_gram)
    narrow[:, 0:CHUNK] = chunked(left_low[...])
    narrow[:, CHUNK : 2 * CHUNK] = chunked(right_low[...])
    left_turn = tn(left_low[...], left_basis[...]).astype(BF)
    right_turn = tn(right_basis[...], right_low[...]).astype(BF)
    half_turned = nn(left_turn, moment_low[...]).astype(BF)
    narrow[:, 2 * CHUNK : 3 * CHUNK] = chunked(nn(half_turned, right_turn).astype(BF))
    each(REPLICAS, lambda step: narrow_copy(step).start())
    narrow_in[me] = narrow[me]

    shift = rotation[0]

    def roll(source, rolled, target, copy):
        def one(step):
            there = (me + step) % REPLICAS
            rolled[there] = source[(there + REPLICAS - shift) % REPLICAS]
            copy(step).start()

        each(REPLICAS, one)
        target[me] = source[(me + REPLICAS - shift) % REPLICAS]

    x_own.wait_recv()
    y_pair = {dy: pass_on(beside, YS, index_of(y + dy, x, core)) for dy in (2, 1, 3)}
    to_twin(beside, YS)
    x_pass = {}
    for dy in (2, 1, 3):
        y_own[dy].wait_recv()
        owner = index_of(y - dy, x, core)
        x_pass[dy] = pass_on(owner, XS, beside)
        to_twin(owner, XS)
    each(REPLICAS, lambda step: wide_copy(step).wait_recv())
    roll(wide_in, wide_rolled, wide_out, wide_copy2)
    x_same.wait_recv()
    to_twin(beside, XS)
    for dy in (2, 1, 3):
        y_same[dy].wait_recv()
        to_twin(index_of(y - dy, x, core), YS)
    each(REPLICAS, lambda step: narrow_copy(step).wait_recv())
    roll(narrow_in, narrow_rolled, narrow_out, narrow_copy2)
    for dy in (2, 1, 3):
        y_pair[dy].wait_recv()
        to_twin(index_of(y - dy, x + 1, core), YS)
    for dy in (2, 1, 3):
        x_pass[dy].wait_recv()
        to_twin(index_of(y - dy, x + 1, core), XS)

    for group in (swaps, x_first, y_first, y_second):
        for copy in group.values():
            copy.wait_send()
    x_second.wait_send()
    each(REPLICAS, lambda step: ring_copy(step).wait_send())
    each(COLUMNS, lambda step: column_copy(step).wait_send())
    for copy in twins:
        copy.wait()
    for copy in copies:
        copy.wait_send()
    each(REPLICAS, lambda step: wide_copy(step).wait_send())
    each(REPLICAS, lambda step: narrow_copy(step).wait_send())
    each(REPLICAS, lambda step: wide_copy2(step).wait())
    each(REPLICAS, lambda step: narrow_copy2(step).wait())


def step(arrays, rotation):
    hbm = pl.BlockSpec(memory_space=pl.ANY)
    dma = pltpu.SemaphoreType.DMA
    moved = (REPLICAS, 3 * CHUNK, SIDE)

    def block(dtype):
        return pltpu.VMEM((SIDE, SIDE), dtype)

    arrays = [pltpu.with_memory_space_constraint(array, pltpu.HBM) for array in arrays]
    return pl.pallas_call(
        step_kernel,
        out_shape=(
            pltpu.VMEM((REPLICAS, SIDE, SIDE), BF),
            pltpu.VMEM(moved, BF),
            pltpu.VMEM(moved, BF),
        ),
        in_specs=[hbm] * len(arrays) + [pl.BlockSpec(memory_space=pltpu.SMEM)],
        out_specs=(pl.BlockSpec(memory_space=pltpu.VMEM),) * 3,
        scratch_shapes=[
            pltpu.VMEM((8, SIDE, SIDE), BF),
            pltpu.VMEM((8, SIDE, SIDE), BF),
            pltpu.VMEM((4, X_ROWS, SIDE), BF),
            pltpu.VMEM((3, 2, Y_ROWS, SIDE), BF),
            pltpu.VMEM((3, X_ROWS, SIDE), BF),
            pltpu.VMEM((Y_ROWS, SIDE), BF),
            pltpu.VMEM((REPLICAS, 8, 128), F32),
            pltpu.VMEM((COLUMNS, 8, 128), F32),
            block(F32),
            block(F32),
            block(F32),
            block(BF),
            block(BF),
            block(BF),
            block(BF),
            block(BF),
            block(F32),
            block(BF),
            block(F32),
            block(F32),
            block(BF),
            block(BF),
            block(BF),
            block(BF),
        ]
        + [pltpu.VMEM(moved, BF)] * 6
        + [dma((8,)), dma((7,)), dma((8,)), dma((8,)), dma((14,)), dma((14,))]
        + [dma((REPLICAS,))] * 2
        + [dma((COLUMNS,))] * 2
        + [dma((14,))] * 2
        + [dma((15,))] * 2
        + [dma((REPLICAS,))] * 8,
        compiler_params=pltpu.CompilerParams(
            collective_id=0, has_side_effects=True, vmem_limit_bytes=46 * 2**20
        ),
        cost_estimate=pl.CostEstimate(
            flops=10**10, bytes_accessed=32 * 2**20, transcendentals=0
        ),
        name="soap_step",
    )(*arrays, rotation)


def finish_kernel(params, wide, narrow, params_out, left, right, second, *rest):
    left_basis, right_basis, first, staged, sems = rest
    copies = [pltpu.make_async_copy(params, params_out, sems.at[0])]
    for k, target in enumerate((left_basis, right_basis, first)):
        copies.append(
            pltpu.make_async_copy(
                narrow.at[:, pl.ds(CHUNK * k, CHUNK)], target, sems.at[1 + k]
            )
        )
    for copy in copies:
        copy.start()
    for k, target in enumerate((left, right, second)):
        staged[k] = wide[:, CHUNK * k : CHUNK * (k + 1)].astype(F32)
        copies.append(pltpu.make_async_copy(staged.at[k], target, sems.at[4 + k]))
        copies[-1].start()
    for copy in copies:
        copy.wait()


def finish(params, wide, narrow):
    hbm = pl.BlockSpec(memory_space=pl.ANY)
    vmem = pl.BlockSpec(memory_space=pltpu.VMEM)
    slots = (REPLICAS, CHUNK, SIDE)
    return pl.pallas_call(
        finish_kernel,
        out_shape=(pltpu.HBM((REPLICAS, SIDE, SIDE), BF),)
        + (pltpu.HBM(slots, F32),) * 3
        + (pltpu.HBM(slots, BF),) * 3,
        in_specs=[vmem, vmem, vmem],
        out_specs=(hbm,) * 7,
        scratch_shapes=[
            pltpu.VMEM((3,) + slots, F32),
            pltpu.SemaphoreType.DMA((7,)),
        ],
        compiler_params=pltpu.CompilerParams(vmem_limit_bytes=24 * 2**20),
        cost_estimate=pl.CostEstimate(flops=0, bytes_accessed=24 * 2**20, transcendentals=0),
        name="finish",
    )(params, wide, narrow)


def local(
    grads,
    left_factor,
    right_factor,
    left_basis,
    right_basis,
    first_moment,
    second_moment,
    parameters,
    rotation,
):
    blocks = (
        left_factor,
        right_factor,
        second_moment,
        left_basis,
        right_basis,
        first_moment,
        parameters,
    )
    params, wide, narrow = step([grads[0, :, 0]] + [value[0, 0] for value in blocks], rotation)
    gathered, *outs = finish(params, wide, narrow)
    left, right, second, left_turned, right_turned, first = (
        value.reshape(1, 1, SIDE, SIDE) for value in outs
    )
    return (gathered[:, None], left, right, left_turned, right_turned, first, second)


def solution(mesh):
    state = P("dp", "fsdp", None, None)
    return jax.shard_map(
        local,
        mesh=mesh,
        in_specs=(P("dp", None, "fsdp", None, None),) + (state,) * 7 + (P("fsdp"),),
        out_specs=(P(None, "fsdp", None, None),) + (state,) * 6,
        check_vma=False,
    )
```

time: 267 us -> 166 us (0.62)
  matrix products: 73.9 us -> 0 us
  local copies, waits for them, and re-layouts: 13.6 us -> 0 us
  other arithmetic: 8.71 us -> 0 us
  between operations: 7.69 us -> 1.45 us
    dot_general x22 -> x0, matrix products: 73.9 us -> none  [dot(): return jnp.dot(a, b, preferred_element_type=F32)]
    unnamed x20 -> x0, local copies, waits for them, and re-layouts: 12.2 us -> none
    reduce_max x8 -> x0, other arithmetic: 4.8 us -> none  [the longest x4 2.41 us: orthonormal(): jnp.max(jnp.sum(magnitude, axis=0)) * jnp.max(jnp.sum(magnitude, axis=1))]
    convert_element_type x3 -> x0, other arithmetic: 3.31 us -> none  [the longest x1 1.1 us: local(): outs[2].astype(F32)]
where the time goes in v2:
time: 166 us; the launch traced here: 165 us
  Pallas kernels  164 us (99%)
    pallas_call x1, Pallas kernels, step(): pl.pallas_call(step_kernel, out_shape=(pltpu.VMEM((REPLICAS, SIDE, SIDE),...  159 us
    pallas_call x1, Pallas kernels, finish(): pl.pallas_call(finish_kernel, out_shape=(pltpu.HBM((REPLICAS, SIDE, SIDE)...  4.9 us

profile of v2, /device:TPU:1, one launch (start us, length us, event | category | flops | bytes accessed | tf_op | source)
XLA Modules:
  0.0 165.4 jit_solution(2174300460063528894)
XLA Ops:
  1.3 159.1 %soap_step.1 = (bf16[16,512,512]{2,1,0:T(8,128)(2,1)S(1)}, bf16[16,96,512]{2,1,0:T(8,128)(2,1)S(1)}, bf16[16,96,512]{2,1,0:T(8,128)(2,1)S(1)}) custom-call(bf16[16,512,512]{2,1,0:T(8,128)(2,1)} %bitcast.17, f32[512,512]{1,0:T(8,128)} %bitcast.19, f32[512,512]{1,0:T(8,128)} %bitcast.20, f32[512,512]{1,0:T(8,128)} %bitcast.21, bf16[512,512]{1,0:T(8,128)(2,1)} %bitcast.25, ...), custom_call_target="tpu_custom_call" | custom-call | flops 10000000000 | bytes 33554432 | tf_op jit(solution)/shard_map/soap_step/pallas_call | solution.py:462
  160.4 4.9 %finish.1 = (bf16[16,512,512]{2,1,0:T(8,128)(2,1)}, f32[16,32,512]{2,1,0:T(8,128)}, f32[16,32,512]{2,1,0:T(8,128)}, f32[16,32,512]{2,1,0:T(8,128)}, bf16[16,32,5...) custom-call(bf16[16,512,512]{2,1,0:T(8,128)(2,1)S(1)} %get-tuple-element.17.params, ...), custom_call_target="tpu_custom_call" | custom-call | bytes 25165824 | tf_op jit(solution)/shard_map/finish/pallas_call | solution.py:537

commit v3 on v2

--- a/solution.py
+++ b/solution.py
@@ -21,10 +21,15 @@
 CLIP_RMS = 0.3
 TINY = 1e-08
 
-Y_ROWS = 208
-X_ROWS = SIDE - Y_ROWS
-YS = pl.ds(0, Y_ROWS)
-XS = pl.ds(Y_ROWS, X_ROWS)
+A_HALF = 144
+A_ROWS = 2 * A_HALF
+B_ROWS = SIDE - A_ROWS
+B_HALF = B_ROWS // 2
+A = pl.ds(0, A_ROWS)
+B = pl.ds(A_ROWS, B_ROWS)
+A0, A1 = pl.ds(0, A_HALF), pl.ds(A_HALF, A_HALF)
+B0, B1 = pl.ds(A_ROWS, B_HALF), pl.ds(A_ROWS + B_HALF, B_HALF)
+LATE0, LATE1 = pl.ds(0, B_HALF), pl.ds(B_HALF, B_HALF)
 
 MESH = pl.DeviceIdType.MESH
 BF = jnp.bfloat16
@@ -111,7 +116,9 @@
     own,
     twin,
     x_in,
+    y_relay,
     y_in,
+    late_relay,
     y_late,
     x_late,
     tile,
@@ -132,9 +139,14 @@
     right_low,
     left_gram,
     right_gram,
+    left_factor,
+    old,
+    outer,
+    old_in,
+    outer_in,
     wide,
+    wide_in,
     narrow,
-    wide_in,
     narrow_in,
     wide_rolled,
     narrow_rolled,
@@ -152,6 +164,12 @@
     ag_recv,
     twin_send,
     twin_recv,
+    old_send,
+    old_recv,
+    old_send2,
+    old_recv2,
+    outer_send,
+    outer_recv,
     wide_send,
     wide_recv,
     wide_send2,
@@ -173,8 +191,14 @@
 
     lax.fori_loop(1, COLUMNS, greet_column, 0)
 
-    order = [(2, 1), (1, 1), (3, 1), (0, 1), (2, 0), (1, 0), (3, 0), (0, 0)]
+    beside = index_of(y, x + 1, core)
+    other = index_of(y, x, core + 1)
+    up = index_of(y + 1, x, core)
+    down = index_of(y - 1, x, core)
+    order = [(2, 1), (2, 0), (1, 1), (3, 1), (1, 0), (3, 0), (0, 1), (0, 0)]
     loads, swaps = {}, {}
+    left_load = pltpu.make_async_copy(left_hbm, left_old, load_sem.at[0])
+    left_load.start()
     for dy, dx in order:
         k = dy * 2 + dx
         loads[dy, dx] = pltpu.make_async_copy(
@@ -189,19 +213,18 @@
             twin.at[k],
             core_send.at[k],
             core_recv.at[k],
-            dp=index_of(y, x, core + 1),
+            dp=other,
         )
         swaps[dy, dx].start()
 
     state_loads = [
-        pltpu.make_async_copy(source, target, load_sem.at[k])
+        pltpu.make_async_copy(source, target, load_sem.at[1 + k])
         for k, (source, target) in enumerate(
             (
                 (left_basis_hbm, left_basis),
                 (right_basis_hbm, right_basis),
                 (first_hbm, first_old),
                 (second_hbm, second_old),
-                (left_hbm, left_old),
                 (right_hbm, right_old),
                 (param_hbm, param_old),
             )
@@ -210,73 +233,112 @@
     for load in state_loads:
         load.start()
 
-    x_first, y_first, y_second = {}, {}, {}
-    used = 0
+    def state_copy(source, target, sends, recvs, step, rows=None):
+        there = (me + step) % REPLICAS
+        if rows is None:
+            return remote(
+                source.at[there], target.at[me], sends.at[step], recvs.at[step], dp=there
+            )
+        return remote(
+            source.at[there, rows], target.at[me, rows], sends.at[step], recvs.at[step], dp=there
+        )
+
+    def old_copy(step):
+        return state_copy(old, old_in, old_send, old_recv, step, pl.ds(0, CHUNK // 2))
+
+    def old_copy2(step):
+        rows = pl.ds(CHUNK // 2, CHUNK // 2)
+        return state_copy(old, old_in, old_send2, old_recv2, step, rows)
+
+    def outer_copy(step):
+        return state_copy(outer, outer_in, outer_send, outer_recv, step)
+
+    left_load.wait()
+    old[...] = chunked(left_old[...].astype(BF))
+    each(REPLICAS, lambda step: old_copy(step).start())
+    old_in[me] = old[me]
+
+    links = []
+
+    def link(source, target, device):
+        k = len(links)
+        copy = remote(source, target, send.at[k], recv.at[k], dp=device)
+        copy.start()
+        links.append(copy)
+        return copy
+
+    def add(k, rows, value):
+        own[k, rows] = own[k, rows] + value
+
+    x_first, far_up, far_down, free_up, free_down, near_up, near_down = ({} for _ in range(7))
     for dy, dx in order:
         k = dy * 2 + dx
         loads[dy, dx].wait()
         swaps[dy, dx].wait_recv()
         own[k] = own[k] + twin[k]
         if dx == 1:
-            x_first[dy] = remote(
-                own.at[k, XS], x_in.at[dy], send.at[used], recv.at[used], dp=index_of(y, x + 1, core)
-            )
-            x_first[dy].start()
-            used += 1
-        if dy:
-            y_first[dy, dx] = remote(
-                own.at[k, YS],
-                y_in.at[dy - 1, dx],
-                send.at[used],
-                recv.at[used],
-                dp=index_of(y + dy, x, core),
-            )
-            y_first[dy, dx].start()
-            used += 1
-    for dy in (2, 1, 3):
-        x_first[dy].wait_recv()
-        own[dy * 2, XS] = own[dy * 2, XS] + x_in[dy]
-        y_second[dy] = remote(
-            own.at[dy * 2, XS],
-            y_late.at[dy - 1],
-            send.at[used],
-            recv.at[used],
-            dp=index_of(y + dy, x, core),
-        )
-        y_second[dy].start()
-        used += 1
-    for dy in (2, 1, 3):
-        y_first[dy, 1].wait_recv()
-    own[1, YS] = (
-        (own[1, YS].astype(F32) + y_in[0, 1].astype(F32))
-        + (y_in[1, 1].astype(F32) + y_in[2, 1].astype(F32))
+            x_first[dy] = link(own.at[k, B], x_in.at[dy], beside)
+        if dy == 2:
+            far_up[dx] = link(own.at[k, A0], y_relay.at[0, dx], up)
+            far_down[dx] = link(own.at[k, A1], y_relay.at[1, dx], down)
+        if dy == 1:
+            free_up[dx] = link(own.at[k, A1], y_in.at[0, dx, A1], up)
+        if dy == 3:
+            free_down[dx] = link(own.at[k, A0], y_in.at[1, dx, A0], down)
+
+    def relay_rows(dx):
+        far_up[dx].wait_recv()
+        add(2 + dx, A0, y_relay[0, dx])
+        near_up[dx] = link(own.at[2 + dx, A0], y_in.at[0, dx, A0], up)
+        far_down[dx].wait_recv()
+        add(6 + dx, A1, y_relay[1, dx])
+        near_down[dx] = link(own.at[6 + dx, A1], y_in.at[1, dx, A1], down)
+
+    relay_rows(1)
+    x_first[2].wait_recv()
+    add(4, B, x_in[2])
+    late_far_up = link(own.at[4, B0], late_relay.at[0], up)
+    late_far_down = link(own.at[4, B1], late_relay.at[1], down)
+    relay_rows(0)
+    x_first[1].wait_recv()
+    add(2, B, x_in[1])
+    late_free_up = link(own.at[2, B1], y_late.at[0, LATE1], up)
+    x_first[3].wait_recv()
+    add(6, B, x_in[3])
+    late_free_down = link(own.at[6, B0], y_late.at[1, LATE0], down)
+    for group in (free_up, near_up, free_down, near_down):
+        group[1].wait_recv()
+    own[1, A] = (
+        own[1, A].astype(F32) + (y_in[0, 1].astype(F32) + y_in[1, 1].astype(F32))
     ).astype(BF)
-    x_second = remote(
-        own.at[1, YS], x_late, send.at[used], recv.at[used], dp=index_of(y, x + 1, core)
-    )
-    x_second.start()
-    for dy in (2, 1, 3):
-        y_first[dy, 0].wait_recv()
+    x_second = link(own.at[1, A], x_late, beside)
+    late_far_up.wait_recv()
+    add(2, B0, late_relay[0])
+    late_near_up = link(own.at[2, B0], y_late.at[0, LATE0], up)
+    late_far_down.wait_recv()
+    add(6, B1, late_relay[1])
+    late_near_down = link(own.at[6, B1], y_late.at[1, LATE1], down)
+    each(REPLICAS, lambda step: old_copy2(step).start())
+    for group in (free_up, near_up, free_down, near_down):
+        group[0].wait_recv()
     x_first[0].wait_recv()
-    for dy in (2, 1, 3):
-        y_second[dy].wait_recv()
-    mean_x = (
-        (own[0, XS].astype(F32) + x_in[0].astype(F32))
-        + (y_late[0].astype(F32) + y_late[1].astype(F32))
-        + y_late[2].astype(F32)
-    ) * (1.0 / REPLICAS)
-    grad_low[XS] = mean_x.astype(BF)
     x_second.wait_recv()
     mean_y = (
-        (own[0, YS].astype(F32) + x_late[...].astype(F32))
+        (own[0, A].astype(F32) + x_late[...].astype(F32))
         + (y_in[0, 0].astype(F32) + y_in[1, 0].astype(F32))
-        + y_in[2, 0].astype(F32)
     ) * (1.0 / REPLICAS)
-    grad_low[YS] = mean_y.astype(BF)
-    squares = jnp.sum((mean_x * mean_x).reshape(X_ROWS // 8, 8, SIDE), axis=0) + jnp.sum(
-        (mean_y * mean_y).reshape(Y_ROWS // 8, 8, SIDE), axis=0
+    grad_low[A] = mean_y.astype(BF)
+    for copy in (late_free_up, late_near_up, late_free_down, late_near_down):
+        copy.wait_recv()
+    mean_x = (
+        (own[0, B].astype(F32) + x_in[0].astype(F32))
+        + (y_late[0].astype(F32) + y_late[1].astype(F32))
+    ) * (1.0 / REPLICAS)
+    grad_low[B] = mean_x.astype(BF)
+    squares = jnp.sum((mean_x * mean_x).reshape(B_ROWS // 8, 8, SIDE), axis=0) + jnp.sum(
+        (mean_y * mean_y).reshape(A_ROWS // 8, 8, SIDE), axis=0
     )
-    tile[0] = (squares[:, :128] + squares[:, 128:256]) + (squares[:, 256:384] + squares[:, 384:])
+    tile2[0] = (squares[:, :128] + squares[:, 128:256]) + (squares[:, 256:384] + squares[:, 384:])
 
     def ring_copy(step):
         return remote(
@@ -296,27 +358,25 @@
             fsdp=(column + step) % COLUMNS,
         )
 
-    each(REPLICAS, lambda step: ring_copy(step).start())
+    each(COLUMNS, lambda step: column_copy(step).start())
+    outer_left = nt(grad_low[...], grad_low[...])
+    left_iter[...] = outer_left
+    outer[...] = chunked(outer_left.astype(BF))
+    outer_in[me] = outer[me]
     for load in state_loads:
         load.wait()
     half_left = tn(left_basis[...], grad_low[...]).astype(BF)
+    each(COLUMNS, lambda step: column_copy(step).wait_recv())
+    tile[0] = jnp.sum(tile2[...], axis=0)
+    each(REPLICAS, lambda step: ring_copy(step).start())
+    each(REPLICAS, lambda step: outer_copy(step).start())
     rotated[...] = nn(half_left, right_basis[...])
+    right_iter[...] = tn(grad_low[...], grad_low[...])
     each(REPLICAS, lambda step: ring_copy(step).wait_recv())
-    tile2[0] = jnp.sum(tile[...], axis=0)
-    each(COLUMNS, lambda step: column_copy(step).start())
-    left_iter[...] = nt(grad_low[...], grad_low[...])
-    right_iter[...] = tn(grad_low[...], grad_low[...])
-    each(COLUMNS, lambda step: column_copy(step).wait_recv())
-    square_sum = jnp.sum(jnp.sum(tile2[...], axis=0))
+    square_sum = jnp.sum(jnp.sum(tile[...], axis=0))
     entries = SIDE * SIDE * REPLICAS * COLUMNS
     clip_factor = jnp.minimum(1.0, CLIP_RMS * math.sqrt(entries) / jnp.sqrt(square_sum + 1e-06))
 
-    def state_copy(source, target, sends, recvs, step):
-        there = (me + step) % REPLICAS
-        return remote(
-            source.at[there], target.at[me], sends.at[step], recvs.at[step], dp=there
-        )
-
     def wide_copy(step):
         return state_copy(wide, wide_in, wide_send, wide_recv, step)
 
@@ -330,61 +390,57 @@
         return state_copy(narrow_rolled, narrow_out, narrow_send2, narrow_recv2, step)
 
     weight = (1.0 - BETA_FACTOR) * (clip_factor * clip_factor)
-    left_new = (BETA_FACTOR * left_old[...] + weight * left_iter[...]).astype(BF)
-    right_new = (BETA_FACTOR * right_old[...] + weight * right_iter[...]).astype(BF)
-    wide[:, 0:CHUNK] = chunked(left_new)
-    wide[:, CHUNK : 2 * CHUNK] = chunked(right_new)
     turned = clip_factor * rotated[...]
     moment = BETA_MOMENT * first_old[...].astype(F32) + (1.0 - BETA_MOMENT) * turned
     second_new = BETA_SECOND * second_old[...] + (1.0 - BETA_SECOND) * turned * turned
-    wide[:, 2 * CHUNK : 3 * CHUNK] = chunked(second_new.astype(BF))
+    wide[:, CHUNK : 2 * CHUNK] = chunked(second_new.astype(BF))
     moment_low[...] = moment.astype(BF)
     direction = (moment / (jnp.sqrt(second_new) + TINY)).astype(BF)
-    each(REPLICAS, lambda step: wide_copy(step).start())
-    wide_in[me] = wide[me]
-
     half_back = nn(left_basis[...], direction).astype(BF)
     update = nt(half_back, right_basis[...])
     params_out[me] = (param_old[...].astype(F32) - STEP_RATE * update).astype(BF)
 
-    beside = index_of(y, x + 1, core)
-    other = index_of(y, x, core + 1)
-    counts = [0, 0]
-    copies = []
+    far = index_of(y + 2, x, core)
+    beside_down = index_of(y - 1, x + 1, core)
+    beside_up = index_of(y + 1, x + 1, core)
+    beside_far = index_of(y + 2, x + 1, core)
+    copies, twins = [], []
 
     def pass_on(owner, rows, target):
-        k = counts[0]
-        counts[0] += 1
+        k = len(copies)
         view = params_out.at[owner, rows]
         copy = remote(view, view, ag_send.at[k], ag_recv.at[k], dp=target)
         copy.start()
         copies.append(copy)
         return copy
 
-    twins = []
-
     def to_twin(owner, rows):
-        k = counts[1]
-        counts[1] += 1
+        k = len(twins)
         view = params_out.at[owner, rows]
         copy = remote(view, view, twin_send.at[k], twin_recv.at[k], dp=other)
         copy.start()
         twins.append(copy)
 
-    x_own = pass_on(me, YS, beside)
-    y_own = {dy: pass_on(me, XS, index_of(y + dy, x, core)) for dy in (2, 1, 3)}
-    x_same = pass_on(me, XS, beside)
-    y_same = {dy: pass_on(me, YS, index_of(y + dy, x, core)) for dy in (2, 1, 3)}
+    x_own = pass_on(me, A, beside)
+    b_up = pass_on(me, B, up)
+    b_down = pass_on(me, B, down)
+    a_up = pass_on(me, A, up)
+    a_down = pass_on(me, A, down)
+    x_same = pass_on(me, B, beside)
     to_twin(me, pl.ds(0, SIDE))
+
+    right_new = (BETA_FACTOR * right_old[...] + weight * right_iter[...]).astype(BF)
+    wide[:, 0:CHUNK] = chunked(right_new)
+    each(REPLICAS, lambda step: wide_copy(step).start())
+    wide_in[me] = wide[me]
+    left_factor[...] = (BETA_FACTOR * left_old[...] + weight * left_iter[...]).astype(BF)
 
     for repeat in range(ITERS):
         left_start = left_basis if repeat == 0 else left_low
         right_start = right_basis if repeat == 0 else right_low
+        image_step(left_factor[...], left_start[...], left_iter, left_low)
         image_step(
-            wide[:, 0:CHUNK].reshape(SIDE, SIDE), left_start[...], left_iter, left_low
-        )
-        image_step(
-            wide[:, CHUNK : 2 * CHUNK].reshape(SIDE, SIDE), right_start[...], right_iter, right_low
+            wide[:, 0:CHUNK].reshape(SIDE, SIDE), right_start[...], right_iter, right_low
         )
         for newton in range(NEWTON):
             newton_step(left_iter, left_low, left_gram)
@@ -395,56 +451,101 @@
     right_turn = tn(right_basis[...], right_low[...]).astype(BF)
     half_turned = nn(left_turn, moment_low[...]).astype(BF)
     narrow[:, 2 * CHUNK : 3 * CHUNK] = chunked(nn(half_turned, right_turn).astype(BF))
+    narrow_in[me] = narrow[me]
+    shift = rotation[0]
+
+    def roll_wide(slot):
+        source = (slot + REPLICAS - shift) % REPLICAS
+        left = BETA_FACTOR * old_in[source].astype(F32) + weight * outer_in[source].astype(F32)
+        return left.astype(BF), wide_in[source]
+
+    def gather_second():
+        x_own.wait_recv()
+        steps = [pass_on(beside, A, up), pass_on(beside, A, down)]
+        to_twin(beside, A)
+        b_up.wait_recv()
+        steps += [pass_on(down, B0, up), pass_on(down, B, beside)]
+        to_twin(down, B)
+        b_down.wait_recv()
+        steps += [pass_on(up, B1, down), pass_on(up, B, beside)]
+        to_twin(up, B)
+        a_up.wait_recv()
+        steps += [pass_on(down, A0, up)]
+        to_twin(down, A)
+        a_down.wait_recv()
+        steps += [pass_on(up, A1, down)]
+        to_twin(up, A)
+        x_same.wait_recv()
+        to_twin(beside, B)
+        return steps
+
+    def gather_third(steps):
+        beside_a_up, beside_a_down, b_far0, b_x_down, b_far1, b_x_up, a_far0, a_far1 = steps
+        b_far0.wait_recv()
+        b_x_far0 = pass_on(far, B0, beside)
+        to_twin(far, B0)
+        b_far1.wait_recv()
+        b_x_far1 = pass_on(far, B1, beside)
+        to_twin(far, B1)
+        beside_a_up.wait_recv()
+        beside_far0 = pass_on(beside_down, A0, up)
+        to_twin(beside_down, A)
+        beside_a_down.wait_recv()
+        beside_far1 = pass_on(beside_up, A1, down)
+        to_twin(beside_up, A)
+        a_far0.wait_recv()
+        to_twin(far, A0)
+        a_far1.wait_recv()
+        to_twin(far, A1)
+        b_x_down.wait_recv()
+        to_twin(beside_down, B)
+        b_x_up.wait_recv()
+        to_twin(beside_up, B)
+        return b_x_far0, b_x_far1, beside_far0, beside_far1
+
+    def gather_last(steps):
+        for copy, rows in zip(steps, (B0, B1, A0, A1)):
+            copy.wait_recv()
+            to_twin(beside_far, rows)
+
+    def send_wide(step):
+        there = (me + step) % REPLICAS
+        left, others = roll_wide(there)
+        wide_rolled[there, 0:CHUNK] = left
+        wide_rolled[there, CHUNK : 3 * CHUNK] = others
+        wide_copy2(step).start()
+
+    def send_narrow(step):
+        there = (me + step) % REPLICAS
+        narrow_rolled[there] = narrow_in[(there + REPLICAS - shift) % REPLICAS]
+        narrow_copy2(step).start()
+
     each(REPLICAS, lambda step: narrow_copy(step).start())
-    narrow_in[me] = narrow[me]
-
-    shift = rotation[0]
-
-    def roll(source, rolled, target, copy):
-        def one(step):
-            there = (me + step) % REPLICAS
-            rolled[there] = source[(there + REPLICAS - shift) % REPLICAS]
-            copy(step).start()
-
-        each(REPLICAS, one)
-        target[me] = source[(me + REPLICAS - shift) % REPLICAS]
-
-    x_own.wait_recv()
-    y_pair = {dy: pass_on(beside, YS, index_of(y + dy, x, core)) for dy in (2, 1, 3)}
-    to_twin(beside, YS)
-    x_pass = {}
-    for dy in (2, 1, 3):
-        y_own[dy].wait_recv()
-        owner = index_of(y - dy, x, core)
-        x_pass[dy] = pass_on(owner, XS, beside)
-        to_twin(owner, XS)
-    each(REPLICAS, lambda step: wide_copy(step).wait_recv())
-    roll(wide_in, wide_rolled, wide_out, wide_copy2)
-    x_same.wait_recv()
-    to_twin(beside, XS)
-    for dy in (2, 1, 3):
-        y_same[dy].wait_recv()
-        to_twin(index_of(y - dy, x, core), YS)
+    second_steps = gather_second()
+    for copy in (old_copy, old_copy2, outer_copy, wide_copy):
+        each(REPLICAS, lambda step, copy=copy: copy(step).wait_recv())
+    each(REPLICAS, send_wide)
+    left, others = roll_wide(me)
+    wide_out[me, 0:CHUNK] = left
+    wide_out[me, CHUNK : 3 * CHUNK] = others
+    last_steps = gather_third(second_steps)
     each(REPLICAS, lambda step: narrow_copy(step).wait_recv())
-    roll(narrow_in, narrow_rolled, narrow_out, narrow_copy2)
-    for dy in (2, 1, 3):
-        y_pair[dy].wait_recv()
-        to_twin(index_of(y - dy, x + 1, core), YS)
-    for dy in (2, 1, 3):
-        x_pass[dy].wait_recv()
-        to_twin(index_of(y - dy, x + 1, core), XS)
-
-    for group in (swaps, x_first, y_first, y_second):
-        for copy in group.values():
-            copy.wait_send()
-    x_second.wait_send()
+    each(REPLICAS, send_narrow)
+    narrow_out[me] = narrow_in[(me + REPLICAS - shift) % REPLICAS]
+    gather_last(last_steps)
+
+    for copy in swaps.values():
+        copy.wait_send()
+    for copy in links:
+        copy.wait_send()
     each(REPLICAS, lambda step: ring_copy(step).wait_send())
     each(COLUMNS, lambda step: column_copy(step).wait_send())
     for copy in twins:
         copy.wait()
     for copy in copies:
         copy.wait_send()
-    each(REPLICAS, lambda step: wide_copy(step).wait_send())
+    for copy in (old_copy, old_copy2, outer_copy, wide_copy):
+        each(REPLICAS, lambda step, copy=copy: copy(step).wait_send())
     each(REPLICAS, lambda step: narrow_copy(step).wait_send())
     each(REPLICAS, lambda step: wide_copy2(step).wait())
     each(REPLICAS, lambda step: narrow_copy2(step).wait())
@@ -471,10 +572,12 @@
         scratch_shapes=[
             pltpu.VMEM((8, SIDE, SIDE), BF),
             pltpu.VMEM((8, SIDE, SIDE), BF),
-            pltpu.VMEM((4, X_ROWS, SIDE), BF),
-            pltpu.VMEM((3, 2, Y_ROWS, SIDE), BF),
-            pltpu.VMEM((3, X_ROWS, SIDE), BF),
-            pltpu.VMEM((Y_ROWS, SIDE), BF),
+            pltpu.VMEM((4, B_ROWS, SIDE), BF),
+            pltpu.VMEM((2, 2, A_HALF, SIDE), BF),
+            pltpu.VMEM((2, 2, A_ROWS, SIDE), BF),
+            pltpu.VMEM((2, B_HALF, SIDE), BF),
+            pltpu.VMEM((2, B_ROWS, SIDE), BF),
+            pltpu.VMEM((A_ROWS, SIDE), BF),
             pltpu.VMEM((REPLICAS, 8, 128), F32),
             pltpu.VMEM((COLUMNS, 8, 128), F32),
             block(F32),
@@ -494,13 +597,16 @@
             block(BF),
             block(BF),
         ]
-        + [pltpu.VMEM(moved, BF)] * 6
-        + [dma((8,)), dma((7,)), dma((8,)), dma((8,)), dma((14,)), dma((14,))]
+        + [block(BF)]
+        + [pltpu.VMEM((REPLICAS, CHUNK, SIDE), BF)] * 4
+        + [pltpu.VMEM((REPLICAS, 2 * CHUNK, SIDE), BF)] * 2
+        + [pltpu.VMEM(moved, BF)] * 4
+        + [dma((8,)), dma((7,)), dma((8,)), dma((8,)), dma((23,)), dma((23,))]
         + [dma((REPLICAS,))] * 2
         + [dma((COLUMNS,))] * 2
-        + [dma((14,))] * 2
-        + [dma((15,))] * 2
-        + [dma((REPLICAS,))] * 8,
+        + [dma((18,))] * 2
+        + [dma((19,))] * 2
+        + [dma((REPLICAS,))] * 14,
         compiler_params=pltpu.CompilerParams(
             collective_id=0, has_side_effects=True, vmem_limit_bytes=46 * 2**20
         ),

time: 166 us -> 153 us (0.922)
  Pallas kernels: 164 us -> 152 us
    pallas_call x1, Pallas kernels: 159 us -> 147 us  [step(): pl.pallas_call(step_kernel, out_shape=(pltpu.VMEM((REPLICAS, SIDE, SIDE),...]
where the time goes in v3:
time: 153 us
  Pallas kernels  152 us (99%)
    pallas_call x1, Pallas kernels, step(): pl.pallas_call(step_kernel, out_shape=(pltpu.VMEM((REPLICAS, SIDE, SIDE),...  147 us
    pallas_call x1, Pallas kernels, finish(): pl.pallas_call(finish_kernel, out_shape=(pltpu.HBM((REPLICAS, SIDE, SIDE)...  4.9 us

profile of v3, /device:TPU:1, one launch (start us, length us, event | category | flops | bytes accessed | tf_op | source)
XLA Modules:
  0.0 152.9 jit_solution(11043726044166575923)
XLA Ops:
  1.3 146.7 %soap_step.1 = (bf16[16,512,512]{2,1,0:T(8,128)(2,1)S(1)}, bf16[16,96,512]{2,1,0:T(8,128)(2,1)S(1)}, bf16[16,96,512]{2,1,0:T(8,128)(2,1)S(1)}) custom-call(bf16[16,512,512]{2,1,0:T(8,128)(2,1)} %bitcast.17, f32[512,512]{1,0:T(8,128)} %bitcast.19, f32[512,512]{1,0:T(8,128)} %bitcast.20, f32[512,512]{1,0:T(8,128)} %bitcast.21, bf16[512,512]{1,0:T(8,128)(2,1)} %bitcast.25, ...), custom_call_target="tpu_custom_call" | custom-call | flops 10000000000 | bytes 33554432 | tf_op jit(solution)/shard_map/soap_step/pallas_call | solution.py:563
  148.0 4.9 %finish.1 = (bf16[16,512,512]{2,1,0:T(8,128)(2,1)}, f32[16,32,512]{2,1,0:T(8,128)}, f32[16,32,512]{2,1,0:T(8,128)}, f32[16,32,512]{2,1,0:T(8,128)}, bf16[16,32,5...) custom-call(bf16[16,512,512]{2,1,0:T(8,128)(2,1)S(1)} %get-tuple-element.17.params, ...), custom_call_target="tpu_custom_call" | custom-call | bytes 25165824 | tf_op jit(solution)/shard_map/finish/pallas_call | solution.py:643

commit v4 on v3

--- a/solution.py
+++ b/solution.py
@@ -112,7 +112,10 @@
     rotation,
     params_out,
     wide_out,
-    narrow_out,
+    second_out,
+    left_low,
+    right_low,
+    first_out,
     own,
     twin,
     x_in,
@@ -132,24 +135,22 @@
     param_old,
     grad_low,
     rotated,
-    moment_low,
     left_iter,
     right_iter,
-    left_low,
-    right_low,
     left_gram,
     right_gram,
-    left_factor,
-    old,
-    outer,
-    old_in,
-    outer_in,
     wide,
     wide_in,
-    narrow,
-    narrow_in,
     wide_rolled,
-    narrow_rolled,
+    left_in,
+    left_rolled,
+    left_moved,
+    right_in,
+    right_rolled,
+    right_moved,
+    second,
+    second_in,
+    second_rolled,
     local_sem,
     load_sem,
     core_send,
@@ -164,20 +165,22 @@
     ag_recv,
     twin_send,
     twin_recv,
-    old_send,
-    old_recv,
-    old_send2,
-    old_recv2,
-    outer_send,
-    outer_recv,
     wide_send,
     wide_recv,
     wide_send2,
     wide_recv2,
-    narrow_send,
-    narrow_recv,
-    narrow_send2,
-    narrow_recv2,
+    second_send,
+    second_recv,
+    second_send2,
+    second_recv2,
+    left_send,
+    left_recv,
+    left_send2,
+    left_recv2,
+    right_send,
+    right_recv,
+    right_send2,
+    right_recv2,
 ):
     me, y, x, core = place()
     column = lax.axis_index("fsdp")
@@ -197,8 +200,6 @@
     down = index_of(y - 1, x, core)
     order = [(2, 1), (2, 0), (1, 1), (3, 1), (1, 0), (3, 0), (0, 1), (0, 0)]
     loads, swaps = {}, {}
-    left_load = pltpu.make_async_copy(left_hbm, left_old, load_sem.at[0])
-    left_load.start()
     for dy, dx in order:
         k = dy * 2 + dx
         loads[dy, dx] = pltpu.make_async_copy(
@@ -218,13 +219,14 @@
         swaps[dy, dx].start()
 
     state_loads = [
-        pltpu.make_async_copy(source, target, load_sem.at[1 + k])
+        pltpu.make_async_copy(source, target, load_sem.at[k])
         for k, (source, target) in enumerate(
             (
                 (left_basis_hbm, left_basis),
                 (right_basis_hbm, right_basis),
                 (first_hbm, first_old),
                 (second_hbm, second_old),
+                (left_hbm, left_old),
                 (right_hbm, right_old),
                 (param_hbm, param_old),
             )
@@ -233,30 +235,48 @@
     for load in state_loads:
         load.start()
 
-    def state_copy(source, target, sends, recvs, step, rows=None):
+    shift = rotation[0]
+
+    def state_copy(source, target, sends, recvs, step):
         there = (me + step) % REPLICAS
-        if rows is None:
-            return remote(
-                source.at[there], target.at[me], sends.at[step], recvs.at[step], dp=there
-            )
         return remote(
-            source.at[there, rows], target.at[me, rows], sends.at[step], recvs.at[step], dp=there
-        )
-
-    def old_copy(step):
-        return state_copy(old, old_in, old_send, old_recv, step, pl.ds(0, CHUNK // 2))
-
-    def old_copy2(step):
-        rows = pl.ds(CHUNK // 2, CHUNK // 2)
-        return state_copy(old, old_in, old_send2, old_recv2, step, rows)
-
-    def outer_copy(step):
-        return state_copy(outer, outer_in, outer_send, outer_recv, step)
-
-    left_load.wait()
-    old[...] = chunked(left_old[...].astype(BF))
-    each(REPLICAS, lambda step: old_copy(step).start())
-    old_in[me] = old[me]
+            source.at[there], target.at[me], sends.at[step], recvs.at[step], dp=there
+        )
+
+    def send_rolled(source, rolled, target, copy):
+        def one(step):
+            there = (me + step) % REPLICAS
+            rolled[there] = source[(there + REPLICAS - shift) % REPLICAS]
+            copy(step).start()
+
+        each(REPLICAS, one)
+        target[me] = source[(me + REPLICAS - shift) % REPLICAS]
+
+    def left_copy(step):
+        return state_copy(left_basis_hbm, left_in, left_send, left_recv, step)
+
+    def left_copy2(step):
+        return state_copy(left_rolled, left_moved, left_send2, left_recv2, step)
+
+    def right_copy(step):
+        return state_copy(right_basis_hbm, right_in, right_send, right_recv, step)
+
+    def right_copy2(step):
+        return state_copy(right_rolled, right_moved, right_send2, right_recv2, step)
+
+    def wide_copy(step):
+        return state_copy(wide, wide_in, wide_send, wide_recv, step)
+
+    def wide_copy2(step):
+        return state_copy(wide_rolled, wide_out, wide_send2, wide_recv2, step)
+
+    def second_copy(step):
+        return state_copy(second, second_in, second_send, second_recv, step)
+
+    def second_copy2(step):
+        return state_copy(second_rolled, second_out, second_send2, second_recv2, step)
+
+    each(REPLICAS, lambda step: left_copy(step).start())
 
     links = []
 
@@ -318,7 +338,7 @@
     late_far_down.wait_recv()
     add(6, B1, late_relay[1])
     late_near_down = link(own.at[6, B1], y_late.at[1, LATE1], down)
-    each(REPLICAS, lambda step: old_copy2(step).start())
+    each(REPLICAS, lambda step: right_copy(step).start())
     for group in (free_up, near_up, free_down, near_down):
         group[0].wait_recv()
     x_first[0].wait_recv()
@@ -359,45 +379,44 @@
         )
 
     each(COLUMNS, lambda step: column_copy(step).start())
-    outer_left = nt(grad_low[...], grad_low[...])
-    left_iter[...] = outer_left
-    outer[...] = chunked(outer_left.astype(BF))
-    outer_in[me] = outer[me]
     for load in state_loads:
         load.wait()
-    half_left = tn(left_basis[...], grad_low[...]).astype(BF)
+    left_in[me] = left_basis[me]
+    right_in[me] = right_basis[me]
+    left_start = left_basis[...].reshape(SIDE, SIDE)
+    right_start = right_basis[...].reshape(SIDE, SIDE)
+    half_left = tn(left_start, grad_low[...]).astype(BF)
+    rotated[...] = nn(half_left, right_start)
     each(COLUMNS, lambda step: column_copy(step).wait_recv())
     tile[0] = jnp.sum(tile2[...], axis=0)
     each(REPLICAS, lambda step: ring_copy(step).start())
-    each(REPLICAS, lambda step: outer_copy(step).start())
-    rotated[...] = nn(half_left, right_basis[...])
+    each(REPLICAS, lambda step: left_copy(step).wait_recv())
+    send_rolled(left_in, left_rolled, left_moved, left_copy2)
+    left_iter[...] = nt(grad_low[...], grad_low[...])
     right_iter[...] = tn(grad_low[...], grad_low[...])
+    each(REPLICAS, lambda step: right_copy(step).wait_recv())
+    send_rolled(right_in, right_rolled, right_moved, right_copy2)
     each(REPLICAS, lambda step: ring_copy(step).wait_recv())
     square_sum = jnp.sum(jnp.sum(tile[...], axis=0))
     entries = SIDE * SIDE * REPLICAS * COLUMNS
     clip_factor = jnp.minimum(1.0, CLIP_RMS * math.sqrt(entries) / jnp.sqrt(square_sum + 1e-06))
 
-    def wide_copy(step):
-        return state_copy(wide, wide_in, wide_send, wide_recv, step)
-
-    def narrow_copy(step):
-        return state_copy(narrow, narrow_in, narrow_send, narrow_recv, step)
-
-    def wide_copy2(step):
-        return state_copy(wide_rolled, wide_out, wide_send2, wide_recv2, step)
-
-    def narrow_copy2(step):
-        return state_copy(narrow_rolled, narrow_out, narrow_send2, narrow_recv2, step)
-
     weight = (1.0 - BETA_FACTOR) * (clip_factor * clip_factor)
     turned = clip_factor * rotated[...]
     moment = BETA_MOMENT * first_old[...].astype(F32) + (1.0 - BETA_MOMENT) * turned
+    wide[:, 2 * CHUNK : 3 * CHUNK] = chunked(moment.astype(BF))
+    left_new = (BETA_FACTOR * left_old[...] + weight * left_iter[...]).astype(BF)
+    right_new = (BETA_FACTOR * right_old[...] + weight * right_iter[...]).astype(BF)
+    wide[:, 0:CHUNK] = chunked(left_new)
+    wide[:, CHUNK : 2 * CHUNK] = chunked(right_new)
+    each(REPLICAS, lambda step: wide_copy(step).start())
+    wide_in[me] = wide[me]
     second_new = BETA_SECOND * second_old[...] + (1.0 - BETA_SECOND) * turned * turned
-    wide[:, CHUNK : 2 * CHUNK] = chunked(second_new.astype(BF))
-    moment_low[...] = moment.astype(BF)
+    second[...] = chunked(second_new.astype(BF))
+    second_in[me] = second[me]
     direction = (moment / (jnp.sqrt(second_new) + TINY)).astype(BF)
-    half_back = nn(left_basis[...], direction).astype(BF)
-    update = nt(half_back, right_basis[...])
+    half_back = nn(left_basis[...].reshape(SIDE, SIDE), direction).astype(BF)
+    update = nt(half_back, right_basis[...].reshape(SIDE, SIDE))
     params_out[me] = (param_old[...].astype(F32) - STEP_RATE * update).astype(BF)
 
     far = index_of(y + 2, x, core)
@@ -428,36 +447,6 @@
     a_down = pass_on(me, A, down)
     x_same = pass_on(me, B, beside)
     to_twin(me, pl.ds(0, SIDE))
-
-    right_new = (BETA_FACTOR * right_old[...] + weight * right_iter[...]).astype(BF)
-    wide[:, 0:CHUNK] = chunked(right_new)
-    each(REPLICAS, lambda step: wide_copy(step).start())
-    wide_in[me] = wide[me]
-    left_factor[...] = (BETA_FACTOR * left_old[...] + weight * left_iter[...]).astype(BF)
-
-    for repeat in range(ITERS):
-        left_start = left_basis if repeat == 0 else left_low
-        right_start = right_basis if repeat == 0 else right_low
-        image_step(left_factor[...], left_start[...], left_iter, left_low)
-        image_step(
-            wide[:, 0:CHUNK].reshape(SIDE, SIDE), right_start[...], right_iter, right_low
-        )
-        for newton in range(NEWTON):
-            newton_step(left_iter, left_low, left_gram)
-            newton_step(right_iter, right_low, right_gram)
-    narrow[:, 0:CHUNK] = chunked(left_low[...])
-    narrow[:, CHUNK : 2 * CHUNK] = chunked(right_low[...])
-    left_turn = tn(left_low[...], left_basis[...]).astype(BF)
-    right_turn = tn(right_basis[...], right_low[...]).astype(BF)
-    half_turned = nn(left_turn, moment_low[...]).astype(BF)
-    narrow[:, 2 * CHUNK : 3 * CHUNK] = chunked(nn(half_turned, right_turn).astype(BF))
-    narrow_in[me] = narrow[me]
-    shift = rotation[0]
-
-    def roll_wide(slot):
-        source = (slot + REPLICAS - shift) % REPLICAS
-        left = BETA_FACTOR * old_in[source].astype(F32) + weight * outer_in[source].astype(F32)
-        return left.astype(BF), wide_in[source]
 
     def gather_second():
         x_own.wait_recv()
@@ -508,30 +497,40 @@
             copy.wait_recv()
             to_twin(beside_far, rows)
 
-    def send_wide(step):
-        there = (me + step) % REPLICAS
-        left, others = roll_wide(there)
-        wide_rolled[there, 0:CHUNK] = left
-        wide_rolled[there, CHUNK : 3 * CHUNK] = others
-        wide_copy2(step).start()
-
-    def send_narrow(step):
-        there = (me + step) % REPLICAS
-        narrow_rolled[there] = narrow_in[(there + REPLICAS - shift) % REPLICAS]
-        narrow_copy2(step).start()
-
-    each(REPLICAS, lambda step: narrow_copy(step).start())
+    each(REPLICAS, lambda step: wide_copy(step).wait_recv())
+    send_rolled(wide_in, wide_rolled, wide_out, wide_copy2)
     second_steps = gather_second()
-    for copy in (old_copy, old_copy2, outer_copy, wide_copy):
+    each(REPLICAS, lambda step: second_copy(step).start())
+
+    for copy in (left_copy2, right_copy2, wide_copy2):
         each(REPLICAS, lambda step, copy=copy: copy(step).wait_recv())
-    each(REPLICAS, send_wide)
-    left, others = roll_wide(me)
-    wide_out[me, 0:CHUNK] = left
-    wide_out[me, CHUNK : 3 * CHUNK] = others
+    left_start = left_moved[...].reshape(SIDE, SIDE)
+    right_start = right_moved[...].reshape(SIDE, SIDE)
+    for repeat in range(ITERS):
+        image_step(
+            wide_out[:, 0:CHUNK].reshape(SIDE, SIDE),
+            left_start if repeat == 0 else left_low[...],
+            left_iter,
+            left_low,
+        )
+        image_step(
+            wide_out[:, CHUNK : 2 * CHUNK].reshape(SIDE, SIDE),
+            right_start if repeat == 0 else right_low[...],
+            right_iter,
+            right_low,
+        )
+        for newton in range(NEWTON):
+            newton_step(left_iter, left_low, left_gram)
+            newton_step(right_iter, right_low, right_gram)
+    left_turn = tn(left_low[...], left_start).astype(BF)
+    right_turn = tn(right_start, right_low[...]).astype(BF)
+    moment_low = wide_out[:, 2 * CHUNK : 3 * CHUNK].reshape(SIDE, SIDE)
+    half_turned = nn(left_turn, moment_low).astype(BF)
+    first_out[...] = nn(half_turned, right_turn).astype(BF)
+
     last_steps = gather_third(second_steps)
-    each(REPLICAS, lambda step: narrow_copy(step).wait_recv())
-    each(REPLICAS, send_narrow)
-    narrow_out[me] = narrow_in[(me + REPLICAS - shift) % REPLICAS]
+    each(REPLICAS, lambda step: second_copy(step).wait_recv())
+    send_rolled(second_in, second_rolled, second_out, second_copy2)
     gather_last(last_steps)
 
     for copy in swaps.values():
@@ -544,16 +543,15 @@
         copy.wait()
     for copy in copies:
         copy.wait_send()
-    for copy in (old_copy, old_copy2, outer_copy, wide_copy):
+    for copy in (left_copy, right_copy, wide_copy, second_copy, left_copy2, right_copy2, wide_copy2):
         each(REPLICAS, lambda step, copy=copy: copy(step).wait_send())
-    each(REPLICAS, lambda step: narrow_copy(step).wait_send())
-    each(REPLICAS, lambda step: wide_copy2(step).wait())
-    each(REPLICAS, lambda step: narrow_copy2(step).wait())
+    each(REPLICAS, lambda step: second_copy2(step).wait())
 
 
 def step(arrays, rotation):
     hbm = pl.BlockSpec(memory_space=pl.ANY)
     dma = pltpu.SemaphoreType.DMA
+    slots = (REPLICAS, CHUNK, SIDE)
     moved = (REPLICAS, 3 * CHUNK, SIDE)
 
     def block(dtype):
@@ -565,10 +563,13 @@
         out_shape=(
             pltpu.VMEM((REPLICAS, SIDE, SIDE), BF),
             pltpu.VMEM(moved, BF),
-            pltpu.VMEM(moved, BF),
+            pltpu.VMEM(slots, BF),
+            block(BF),
+            block(BF),
+            block(BF),
         ),
         in_specs=[hbm] * len(arrays) + [pl.BlockSpec(memory_space=pltpu.SMEM)],
-        out_specs=(pl.BlockSpec(memory_space=pltpu.VMEM),) * 3,
+        out_specs=(pl.BlockSpec(memory_space=pltpu.VMEM),) * 6,
         scratch_shapes=[
             pltpu.VMEM((8, SIDE, SIDE), BF),
             pltpu.VMEM((8, SIDE, SIDE), BF),
@@ -583,30 +584,25 @@
             block(F32),
             block(F32),
             block(F32),
-            block(BF),
-            block(BF),
+            pltpu.VMEM(slots, BF),
+            pltpu.VMEM(slots, BF),
             block(BF),
             block(BF),
             block(BF),
             block(F32),
-            block(BF),
             block(F32),
             block(F32),
             block(BF),
             block(BF),
-            block(BF),
-            block(BF),
         ]
-        + [block(BF)]
-        + [pltpu.VMEM((REPLICAS, CHUNK, SIDE), BF)] * 4
-        + [pltpu.VMEM((REPLICAS, 2 * CHUNK, SIDE), BF)] * 2
-        + [pltpu.VMEM(moved, BF)] * 4
+        + [pltpu.VMEM(moved, BF)] * 3
+        + [pltpu.VMEM(slots, BF)] * 9
         + [dma((8,)), dma((7,)), dma((8,)), dma((8,)), dma((23,)), dma((23,))]
         + [dma((REPLICAS,))] * 2
         + [dma((COLUMNS,))] * 2
         + [dma((18,))] * 2
         + [dma((19,))] * 2
-        + [dma((REPLICAS,))] * 14,
+        + [dma((REPLICAS,))] * 16,
         compiler_params=pltpu.CompilerParams(
             collective_id=0, has_side_effects=True, vmem_limit_bytes=46 * 2**20
         ),
@@ -617,44 +613,65 @@
     )(*arrays, rotation)
 
 
-def finish_kernel(params, wide, narrow, params_out, left, right, second, *rest):
-    left_basis, right_basis, first, staged, sems = rest
-    copies = [pltpu.make_async_copy(params, params_out, sems.at[0])]
-    for k, target in enumerate((left_basis, right_basis, first)):
-        copies.append(
-            pltpu.make_async_copy(
-                narrow.at[:, pl.ds(CHUNK * k, CHUNK)], target, sems.at[1 + k]
+def finish_kernel(
+    params,
+    wide,
+    second,
+    left_low,
+    right_low,
+    first,
+    params_out,
+    left_out,
+    right_out,
+    second_out,
+    left_basis_out,
+    right_basis_out,
+    first_out,
+    staged,
+    sems,
+):
+    copies = [
+        pltpu.make_async_copy(source, target, sems.at[k])
+        for k, (source, target) in enumerate(
+            (
+                *(
+                    (params.at[pl.ds(4 * part, 4)], params_out.at[pl.ds(4 * part, 4)])
+                    for part in range(4)
+                ),
+                (left_low, left_basis_out),
+                (right_low, right_basis_out),
+                (first, first_out),
             )
         )
+    ]
     for copy in copies:
         copy.start()
-    for k, target in enumerate((left, right, second)):
-        staged[k] = wide[:, CHUNK * k : CHUNK * (k + 1)].astype(F32)
-        copies.append(pltpu.make_async_copy(staged.at[k], target, sems.at[4 + k]))
+    for k, target in enumerate((left_out, right_out, second_out)):
+        source = second[...] if k == 2 else wide[:, CHUNK * k : CHUNK * (k + 1)]
+        staged[k] = source.astype(F32)
+        copies.append(pltpu.make_async_copy(staged.at[k], target, sems.at[7 + k]))
         copies[-1].start()
     for copy in copies:
         copy.wait()
 
 
-def finish(params, wide, narrow):
-    hbm = pl.BlockSpec(memory_space=pl.ANY)
-    vmem = pl.BlockSpec(memory_space=pltpu.VMEM)
+def finish(arrays):
     slots = (REPLICAS, CHUNK, SIDE)
     return pl.pallas_call(
         finish_kernel,
         out_shape=(pltpu.HBM((REPLICAS, SIDE, SIDE), BF),)
         + (pltpu.HBM(slots, F32),) * 3
-        + (pltpu.HBM(slots, BF),) * 3,
-        in_specs=[vmem, vmem, vmem],
-        out_specs=(hbm,) * 7,
+        + (pltpu.HBM((SIDE, SIDE), BF),) * 3,
+        in_specs=[pl.BlockSpec(memory_space=pltpu.VMEM)] * len(arrays),
+        out_specs=(pl.BlockSpec(memory_space=pl.ANY),) * 7,
         scratch_shapes=[
             pltpu.VMEM((3,) + slots, F32),
-            pltpu.SemaphoreType.DMA((7,)),
+            pltpu.SemaphoreType.DMA((10,)),
         ],
         compiler_params=pltpu.CompilerParams(vmem_limit_bytes=24 * 2**20),
         cost_estimate=pl.CostEstimate(flops=0, bytes_accessed=24 * 2**20, transcendentals=0),
         name="finish",
-    )(params, wide, narrow)
+    )(*arrays)
 
 
 def local(
@@ -677,8 +694,11 @@
         first_moment,
         parameters,
     )
-    params, wide, narrow = step([grads[0, :, 0]] + [value[0, 0] for value in blocks], rotation)
-    gathered, *outs = finish(params, wide, narrow)
+    slots = (REPLICAS, CHUNK, SIDE)
+    arrays = [grads[0, :, 0]] + [value[0, 0] for value in blocks]
+    for k in (4, 5):
+        arrays[k] = arrays[k].reshape(slots)
+    gathered, *outs = finish(step(arrays, rotation))
     left, right, second, left_turned, right_turned, first = (
         value.reshape(1, 1, SIDE, SIDE) for value in outs
     )

time: 153 us -> 145 us (0.948)
  Pallas kernels: 152 us -> 144 us
    pallas_call x1, Pallas kernels: 147 us -> 139 us  [step(): pl.pallas_call(step_kernel, out_shape=(pltpu.VMEM((REPLICAS, SIDE, SIDE),...]
where the time goes in v4:
time: 145 us
  Pallas kernels  144 us (99%)
  between operations  1.45 us (1%)
    pallas_call x1, Pallas kernels, step(): pl.pallas_call(step_kernel, out_shape=(pltpu.VMEM((REPLICAS, SIDE, SIDE),...  139 us
    pallas_call x1, Pallas kernels, finish(): pl.pallas_call(finish_kernel, out_shape=(pltpu.HBM((REPLICAS, SIDE, SIDE)...  4.81 us

profile of v4, /device:TPU:1, one launch (start us, length us, event | category | flops | bytes accessed | tf_op | source)
XLA Modules:
  0.0 145.1 jit_solution(8219526301286098299)
XLA Ops:
  1.3 138.9 %soap_step.1 = (bf16[16,512,512]{2,1,0:T(8,128)(2,1)S(1)}, bf16[16,96,512]{2,1,0:T(8,128)(2,1)S(1)}, bf16[16,32,512]{2,1,0:T(8,128)(2,1)S(1)}, bf16[512,512]{1,0...) custom-call(bf16[16,512,512]{2,1,0:T(8,128)(2,1)} %bitcast.17, f32[512,512]{1,0:T(8,128)} %bitcast.19, ...), custom_call_target="tpu_custom_call" | custom-call | flops 10000000000 | bytes 33554432 | tf_op jit(solution)/shard_map/soap_step/pallas_call | solution.py:561
  140.2 4.8 %finish.1 = (bf16[16,512,512]{2,1,0:T(8,128)(2,1)}, f32[16,32,512]{2,1,0:T(8,128)}, f32[16,32,512]{2,1,0:T(8,128)}, f32[16,32,512]{2,1,0:T(8,128)}, bf16[512,512...) custom-call(bf16[16,512,512]{2,1,0:T(8,128)(2,1)S(1)} %get-tuple-element.20.params, ...), custom_call_target="tpu_custom_call" | custom-call | bytes 25165824 | tf_op jit(solution)/shard_map/finish/pallas_call | solution.py:660

commit v5 on v4

--- a/solution.py
+++ b/solution.py
@@ -173,10 +173,14 @@
     second_recv,
     second_send2,
     second_recv2,
+    left_late_send,
+    left_late_recv,
     left_send,
     left_recv,
     left_send2,
     left_recv2,
+    right_late_send,
+    right_late_recv,
     right_send,
     right_recv,
     right_send2,
@@ -252,14 +256,31 @@
         each(REPLICAS, one)
         target[me] = source[(me + REPLICAS - shift) % REPLICAS]
 
+    def half_copy(source, target, start, sends, recvs, step):
+        there = (me + step) % REPLICAS
+        rows = pl.ds(start, CHUNK // 2)
+        return remote(
+            source.at[there, rows], target.at[me, rows], sends.at[step], recvs.at[step], dp=there
+        )
+
     def left_copy(step):
-        return state_copy(left_basis_hbm, left_in, left_send, left_recv, step)
+        return half_copy(left_basis_hbm, left_in, 0, left_send, left_recv, step)
+
+    def left_late(step):
+        return half_copy(
+            left_basis_hbm, left_in, CHUNK // 2, left_late_send, left_late_recv, step
+        )
 
     def left_copy2(step):
         return state_copy(left_rolled, left_moved, left_send2, left_recv2, step)
 
     def right_copy(step):
-        return state_copy(right_basis_hbm, right_in, right_send, right_recv, step)
+        return half_copy(right_basis_hbm, right_in, 0, right_send, right_recv, step)
+
+    def right_late(step):
+        return half_copy(
+            right_basis_hbm, right_in, CHUNK // 2, right_late_send, right_late_recv, step
+        )
 
     def right_copy2(step):
         return state_copy(right_rolled, right_moved, right_send2, right_recv2, step)
@@ -338,6 +359,7 @@
     late_far_down.wait_recv()
     add(6, B1, late_relay[1])
     late_near_down = link(own.at[6, B1], y_late.at[1, LATE1], down)
+    each(REPLICAS, lambda step: left_late(step).start())
     each(REPLICAS, lambda step: right_copy(step).start())
     for group in (free_up, near_up, free_down, near_down):
         group[0].wait_recv()
@@ -379,6 +401,7 @@
         )
 
     each(COLUMNS, lambda step: column_copy(step).start())
+    each(REPLICAS, lambda step: right_late(step).start())
     for load in state_loads:
         load.wait()
     left_in[me] = left_basis[me]
@@ -390,11 +413,13 @@
     each(COLUMNS, lambda step: column_copy(step).wait_recv())
     tile[0] = jnp.sum(tile2[...], axis=0)
     each(REPLICAS, lambda step: ring_copy(step).start())
-    each(REPLICAS, lambda step: left_copy(step).wait_recv())
+    for copy in (left_copy, left_late):
+        each(REPLICAS, lambda step, copy=copy: copy(step).wait_recv())
     send_rolled(left_in, left_rolled, left_moved, left_copy2)
     left_iter[...] = nt(grad_low[...], grad_low[...])
     right_iter[...] = tn(grad_low[...], grad_low[...])
-    each(REPLICAS, lambda step: right_copy(step).wait_recv())
+    for copy in (right_copy, right_late):
+        each(REPLICAS, lambda step, copy=copy: copy(step).wait_recv())
     send_rolled(right_in, right_rolled, right_moved, right_copy2)
     each(REPLICAS, lambda step: ring_copy(step).wait_recv())
     square_sum = jnp.sum(jnp.sum(tile[...], axis=0))
@@ -543,7 +568,8 @@
         copy.wait()
     for copy in copies:
         copy.wait_send()
-    for copy in (left_copy, right_copy, wide_copy, second_copy, left_copy2, right_copy2, wide_copy2):
+    early = (left_copy, left_late, right_copy, right_late, left_copy2, right_copy2)
+    for copy in early + (wide_copy, second_copy, wide_copy2):
         each(REPLICAS, lambda step, copy=copy: copy(step).wait_send())
     each(REPLICAS, lambda step: second_copy2(step).wait())
 
@@ -602,7 +628,7 @@
         + [dma((COLUMNS,))] * 2
         + [dma((18,))] * 2
         + [dma((19,))] * 2
-        + [dma((REPLICAS,))] * 16,
+        + [dma((REPLICAS,))] * 20,
         compiler_params=pltpu.CompilerParams(
             collective_id=0, has_side_effects=True, vmem_limit_bytes=46 * 2**20
         ),

time: 145 us -> 144 us (level)
  Pallas kernels: 144 us -> 142 us
    pallas_call x1, Pallas kernels: 139 us -> 137 us  [step(): pl.pallas_call(step_kernel, out_shape=(pltpu.VMEM((REPLICAS, SIDE, SIDE),...]
where the time goes in v5:
time: 144 us; the launch traced here: 143 us
  Pallas kernels  142 us (99%)
  between operations  1.45 us (1%)
    pallas_call x1, Pallas kernels, step(): pl.pallas_call(step_kernel, out_shape=(pltpu.VMEM((REPLICAS, SIDE, SIDE),...  137 us
    pallas_call x1, Pallas kernels, finish(): pl.pallas_call(finish_kernel, out_shape=(pltpu.HBM((REPLICAS, SIDE, SIDE)...  4.81 us

profile of v5, /device:TPU:1, one launch (start us, length us, event | category | flops | bytes accessed | tf_op | source)
XLA Modules:
  0.0 143.4 jit_solution(16535649158757357365)
XLA Ops:
  1.3 137.1 %soap_step.1 = (bf16[16,512,512]{2,1,0:T(8,128)(2,1)S(1)}, bf16[16,96,512]{2,1,0:T(8,128)(2,1)S(1)}, bf16[16,32,512]{2,1,0:T(8,128)(2,1)S(1)}, bf16[512,512]{1,0...) custom-call(bf16[16,512,512]{2,1,0:T(8,128)(2,1)} %bitcast.17, f32[512,512]{1,0:T(8,128)} %bitcast.19, ...), custom_call_target="tpu_custom_call" | custom-call | flops 10000000000 | bytes 33554432 | tf_op jit(solution)/shard_map/soap_step/pallas_call | solution.py:587
  138.4 4.8 %finish.1 = (bf16[16,512,512]{2,1,0:T(8,128)(2,1)}, f32[16,32,512]{2,1,0:T(8,128)}, f32[16,32,512]{2,1,0:T(8,128)}, f32[16,32,512]{2,1,0:T(8,128)}, bf16[512,512...) custom-call(bf16[16,512,512]{2,1,0:T(8,128)(2,1)S(1)} %get-tuple-element.20.params, ...), custom_call_target="tpu_custom_call" | custom-call | bytes 25165824 | tf_op jit(solution)/shard_map/finish/pallas_call | solution.py:686

commit v6 on v5

--- a/solution.py
+++ b/solution.py
@@ -190,13 +190,23 @@
     column = lax.axis_index("fsdp")
     barrier = pltpu.get_barrier_semaphore()
     greet_replicas(barrier, me)
-    def greet_column(step, carry):
+    z, x_high = column // 2, column % 2
+
+    def greet(dp, fsdp):
         pl.semaphore_signal(
-            barrier, inc=1, device_id={"fsdp": (column + step) % COLUMNS}, device_id_type=MESH
-        )
+            barrier, inc=1, device_id={"dp": dp, "fsdp": fsdp}, device_id_type=MESH
+        )
+
+    def greet_plane(step, carry):
+        greet(index_of(y + step // 2, x + step, core), z * 2 + (1 - x_high))
         return carry
 
-    lax.fori_loop(1, COLUMNS, greet_column, 0)
+    def greet_line(step, carry):
+        greet(index_of(y, x, core + step), (z + step // 2) % 4 * 2 + x_high)
+        return carry
+
+    lax.fori_loop(0, 8, greet_plane, 0)
+    lax.fori_loop(2, 8, greet_line, 0)
 
     beside = index_of(y, x + 1, core)
     other = index_of(y, x, core + 1)
@@ -210,7 +220,7 @@
             grads.at[index_of(y + dy, x + dx, core)], own.at[k], local_sem.at[k]
         )
         loads[dy, dx].start()
-    pl.semaphore_wait(barrier, REPLICAS - 1 + COLUMNS - 1)
+    pl.semaphore_wait(barrier, REPLICAS - 1 + 14)
     for dy, dx in order:
         k = dy * 2 + dx
         swaps[dy, dx] = remote(
@@ -382,22 +392,26 @@
     )
     tile2[0] = (squares[:, :128] + squares[:, 128:256]) + (squares[:, 256:384] + squares[:, 384:])
 
+    def column_copy(step):
+        there = (z * 2 + core + step) % COLUMNS
+        return remote(
+            tile2.at[0],
+            tile2.at[step],
+            column_send.at[step],
+            column_recv.at[step],
+            dp=index_of(y, x, there % 2),
+            fsdp=there // 2 * 2 + x_high,
+        )
+
     def ring_copy(step):
+        there = (y * 4 + x * 2 + x_high + step) % REPLICAS
         return remote(
             tile.at[0],
             tile.at[step],
             ring_send.at[step],
             ring_recv.at[step],
-            dp=(me + step) % REPLICAS,
-        )
-
-    def column_copy(step):
-        return remote(
-            tile2.at[0],
-            tile2.at[step],
-            column_send.at[step],
-            column_recv.at[step],
-            fsdp=(column + step) % COLUMNS,
+            dp=index_of(there // 4, there // 2, core),
+            fsdp=z * 2 + there % 2,
         )
 
     each(COLUMNS, lambda step: column_copy(step).start())

time: 144 us -> 145 us (level)
  no operation moved by 1% of the time
where the time goes in v6:
time: 145 us; the launch traced here: 144 us
  Pallas kernels  143 us (99%)
  between operations  1.45 us (1%)
    pallas_call x1, Pallas kernels, step(): pl.pallas_call(step_kernel, out_shape=(pltpu.VMEM((REPLICAS, SIDE, SIDE),...  138 us
    pallas_call x1, Pallas kernels, finish(): pl.pallas_call(finish_kernel, out_shape=(pltpu.HBM((REPLICAS, SIDE, SIDE)...  4.81 us

profile of v6, /device:TPU:1, one launch (start us, length us, event | category | flops | bytes accessed | tf_op | source)
XLA Modules:
  0.0 144.3 jit_solution(12716327397237395603)
XLA Ops:
  1.3 138.0 %soap_step.1 = (bf16[16,512,512]{2,1,0:T(8,128)(2,1)S(1)}, bf16[16,96,512]{2,1,0:T(8,128)(2,1)S(1)}, bf16[16,32,512]{2,1,0:T(8,128)(2,1)S(1)}, bf16[512,512]{1,0...) custom-call(bf16[16,512,512]{2,1,0:T(8,128)(2,1)} %bitcast.17, f32[512,512]{1,0:T(8,128)} %bitcast.19, ...), custom_call_target="tpu_custom_call" | custom-call | flops 10000000000 | bytes 33554432 | tf_op jit(solution)/shard_map/soap_step/pallas_call | solution.py:601
  139.3 4.8 %finish.1 = (bf16[16,512,512]{2,1,0:T(8,128)(2,1)}, f32[16,32,512]{2,1,0:T(8,128)}, f32[16,32,512]{2,1,0:T(8,128)}, f32[16,32,512]{2,1,0:T(8,128)}, bf16[512,512...) custom-call(bf16[16,512,512]{2,1,0:T(8,128)(2,1)S(1)} %get-tuple-element.20.params, ...), custom_call_target="tpu_custom_call" | custom-call | bytes 25165824 | tf_op jit(solution)/shard_map/finish/pallas_call | solution.py:700
